TPU v7x, 32 devices: a whole 2x2x4 slice. The times are simulated.
32 devices in a mesh: dp: 2 (over x), fsdp: 16 (over z, y, core).
Axes of the slice: x: 2, y: 2, z: 4, core: 2. Of those that a mesh axis runs over, the one named last changes fastest.
Arguments:
- source: bfloat16 [8192, 512], P(('dp', 'fsdp')), may hold values from -6 to 6
- first_in: bfloat16 [8192, 512], P(('dp', 'fsdp')), may hold values from -6 to 6
- second_in: bfloat16 [8192, 512], P(('dp', 'fsdp')), may hold values from -6 to 6
- cot_first: bfloat16 [8192, 512], P(('dp', 'fsdp')), may hold values from -6 to 6
- cot_second: bfloat16 [8192, 512], P(('dp', 'fsdp')), may hold values from -6 to 6
- src_lengths: int32 [32, 8], P(('dp', 'fsdp')), may hold values from 1 to 128, 256 in all within a row
- tgt_lengths: int32 [32, 8], P(('dp', 'fsdp')), may hold values from 1 to 128, 256 in all within a row
- enc_attn_in: bfloat16 [512, 1536], P('fsdp'), may hold values from -0.25 to 0.25
- enc_attn_out: bfloat16 [512, 512], P('fsdp'), may hold values from -0.75 to 0.75
- enc_ffn_in: bfloat16 [512, 2048], P('fsdp'), may hold values from -0.25 to 0.25
- enc_ffn_out: bfloat16 [2048, 512], P('fsdp'), may hold values from -0.125 to 0.125
- enc_gain: bfloat16 [2, 512], P(None, 'fsdp'), may hold values from 0.5 to 1.5
- enc_bias: bfloat16 [2, 512], P(None, 'fsdp'), may hold values from -3 to 3
- dec_self_in: bfloat16 [512, 1536], P('fsdp'), may hold values from -0.25 to 0.25
- dec_self_out: bfloat16 [512, 512], P('fsdp'), may hold values from -0.75 to 0.75
- dec_cross_q: bfloat16 [512, 512], P('fsdp'), may hold values from -0.25 to 0.25
- dec_cross_kv: bfloat16 [512, 1024], P('fsdp'), may hold values from -0.25 to 0.25
- dec_cross_out: bfloat16 [512, 512], P('fsdp'), may hold values from -0.75 to 0.75
- dec_ffn_in: bfloat16 [512, 2048], P('fsdp'), may hold values from -0.25 to 0.25
- dec_ffn_out: bfloat16 [2048, 512], P('fsdp'), may hold values from -0.125 to 0.125
- dec_gain: bfloat16 [3, 512], P(None, 'fsdp'), may hold values from 0.5 to 1.5
- dec_bias: bfloat16 [3, 512], P(None, 'fsdp'), may hold values from -3 to 3
Outputs:
- first_out: bfloat16 [8192, 512], P(('dp', 'fsdp'))
- second_out: bfloat16 [8192, 512], P(('dp', 'fsdp'))
- source_grad: float32 [8192, 512], P(('dp', 'fsdp'))
- first_grad: float32 [8192, 512], P(('dp', 'fsdp'))
- enc_attn_in_grad: float32 [512, 1536], P('fsdp')
- enc_attn_out_grad: float32 [512, 512], P('fsdp')
- enc_ffn_in_grad: float32 [512, 2048], P('fsdp')
- enc_ffn_out_grad: float32 [2048, 512], P('fsdp')
- enc_gain_grad: float32 [2, 512], P(None, 'fsdp')
- enc_bias_grad: float32 [2, 512], P(None, 'fsdp')
- dec_self_in_grad: float32 [512, 1536], P('fsdp')
- dec_self_out_grad: float32 [512, 512], P('fsdp')
- dec_cross_q_grad: float32 [512, 512], P('fsdp')
- dec_cross_kv_grad: float32 [512, 1024], P('fsdp')
- dec_cross_out_grad: float32 [512, 512], P('fsdp')
- dec_ffn_in_grad: float32 [512, 2048], P('fsdp')
- dec_ffn_out_grad: float32 [2048, 512], P('fsdp')
- dec_gain_grad: float32 [3, 512], P(None, 'fsdp')
- dec_bias_grad: float32 [3, 512], P(None, 'fsdp')
Inputs may be any that keep to these rules, and one draw needn't show every extreme that they name: `src_lengths`: row r lists in order the lengths of the 8 source sentences that fill tokens r * 256 to (r + 1) * 256 - 1 of source; they sum to 256; sentence k of a row pairs with sentence k of the same row of tgt_lengths. `tgt_lengths`: row r lists in order the lengths of the 8 target sentences that fill tokens r * 256 to (r + 1) * 256 - 1 of first_in, second_in and the cotangents; they sum to 256.
All inputs are finite; a program needn't handle non-finite values.
Results may differ from a plain program's by a relative error of at most 0.029.
Values may be sent and summed in bfloat16 or wider, within the bound.
No kernel may reach another device: no remote copies, remote signals or barrier semaphores. Data moves between devices by JAX's collectives and lax.ppermute only.
A program may use at most 192 MiB of HBM per device.

v0:
```python
import functools
import typing

import jax
import jax.numpy as jnp
from jax import lax
from jax.experimental import pallas as pl
from jax.experimental.pallas import tpu as pltpu
from jax.sharding import PartitionSpec as P

D = 512
HEADS = 8
HEAD = 64
TOK = 256
FF = 2048
QUAD = 256
BLOCK = 32
EPSILON = 1e-05
MASKED = -1000000000.0
BF = jnp.bfloat16
F32 = jnp.float32
VMEM_LIMIT = 64 * 1024 * 1024
COST = 1.1e9


class Layout(typing.NamedTuple):
    offset: int
    pieces: int
    made: int = 2
    made_offset: int = 0
    made_rows: int = 0


def dot(left, right):
    return lax.dot_general(left, right, (((1,), (0,)), ((), ())), preferred_element_type=F32)


def dot_nt(left, right):
    return lax.dot_general(left, right, (((1,), (1,)), ((), ())), preferred_element_type=F32)


def dot_tn(left, right):
    return lax.dot_general(left, right, (((0,), (0,)), ((), ())), preferred_element_type=F32)


def wait_all(copies):
    for copy in copies:
        copy.wait()


def column_block(held, index):
    return held[:, :, index * BLOCK : (index + 1) * BLOCK].reshape(D, D)


def row_block(held, index):
    return held[index, :, 4 * BLOCK : 8 * BLOCK].reshape(D, D)


def normed_of(values):
    centre = values - jnp.mean(values, axis=-1, keepdims=True)
    spread = jnp.mean(centre * centre, axis=-1, keepdims=True)
    inverse = lax.rsqrt(spread + EPSILON)
    return centre * inverse, inverse


def norm_back(unit, inverse, gain, grad_normed, norm_ref):
    norm_ref[0:1] = jnp.sum(grad_normed * unit, axis=0, keepdims=True)
    norm_ref[1:2] = jnp.sum(grad_normed, axis=0, keepdims=True)
    grad_unit = grad_normed * gain
    return (
        grad_unit
        - jnp.mean(grad_unit, axis=-1, keepdims=True)
        - unit * jnp.mean(grad_unit * unit, axis=-1, keepdims=True)
    ) * inverse


def mask_bias(key_lengths, query_lengths):
    key_place = lax.broadcasted_iota(jnp.int32, (TOK, 1), 0)
    query_place = lax.broadcasted_iota(jnp.int32, (1, TOK), 1)
    key_ids = jnp.zeros((TOK, 1), jnp.int32)
    query_ids = jnp.zeros((1, TOK), jnp.int32)
    key_end = jnp.int32(0)
    query_end = jnp.int32(0)
    for k in range(key_lengths.shape[1]):
        key_end = key_end + key_lengths[0, k]
        query_end = query_end + query_lengths[0, k]
        key_ids = key_ids + jnp.where(key_place >= key_end, 1, 0)
        query_ids = query_ids + jnp.where(query_place >= query_end, 1, 0)
    return jnp.where(key_ids == query_ids, 0.0, MASKED).astype(F32)


def lane_masks():
    head_of = lax.broadcasted_iota(jnp.int32, (1, QUAD), 1) // HEAD
    return [jnp.where(head_of == h, 1.0, 0.0).astype(BF) for h in range(QUAD // HEAD)]


def attend(queries, keys, values, bias, probs_ref, first):
    masks = lane_masks()
    outs = []
    for g in range(D // QUAD):
        cols = slice(g * QUAD, (g + 1) * QUAD)
        q, k, v = queries[:, cols], keys[:, cols], values[:, cols]
        total = None
        for h in range(QUAD // HEAD):
            scores = dot_nt(k * (masks[h] * (HEAD**-0.5)), q) + bias
            top = jnp.max(scores, axis=0, keepdims=True)
            grown = jnp.exp(scores - top)
            probs = (grown * (1.0 / jnp.sum(grown, axis=0, keepdims=True))).astype(BF)
            probs_ref[first + g * (QUAD // HEAD) + h] = probs
            part = dot_tn(probs, v * masks[h])
            total = part if total is None else total + part
        outs.append(total.astype(BF))
    return jnp.concatenate(outs, axis=1)


def attend_back(queries, keys, values, probs_ref, first, grad_mixed):
    masks = lane_masks()
    grads = []
    for g in range(D // QUAD):
        cols = slice(g * QUAD, (g + 1) * QUAD)
        q, k, v, go = queries[:, cols], keys[:, cols], values[:, cols], grad_mixed[:, cols]
        gq = gk = gv = None
        for h in range(QUAD // HEAD):
            probs_low = probs_ref[first + g * (QUAD // HEAD) + h]
            probs = probs_low.astype(F32)
            grad_probs = dot_nt(v * masks[h], go)
            both = probs * grad_probs
            grad_scores = (both - probs * jnp.sum(both, axis=0, keepdims=True)).astype(BF)
            part_v = dot(probs_low, go * masks[h])
            part_k = dot(grad_scores, q * masks[h])
            part_q = dot_tn(grad_scores, k * masks[h])
            gv = part_v if gv is None else gv + part_v
            gk = part_k if gk is None else gk + part_k
            gq = part_q if gq is None else gq + part_q
        grads.append((gq * (HEAD**-0.5), gk * (HEAD**-0.5), gv))
    return tuple(jnp.concatenate(parts, axis=1) for parts in zip(*grads))


def put_block(held, index, product):
    held[:, :, index * BLOCK : (index + 1) * BLOCK] = product.astype(BF).reshape(4, 4, BLOCK, D)


class Copies:
    def __init__(self, sems):
        self.sems, self.count, self.out = sems, 0, []

    def start(self, source, target):
        copy = pltpu.make_async_copy(source, target, self.sems.at[self.count])
        self.count += 1
        copy.start()
        return copy

    def load(self, source, target):
        return Loaded(target, [self.start(source, target)])

    def store(self, source, target):
        self.out.append(self.start(source, target))

    def finish(self):
        wait_all(self.out)

    def fetch(self, place, pieces, layout, held):
        rows = held.shape[2] // 4
        if layout.pieces == 1:
            loads = []
            for half in range(2):
                part = pieces[0].at[:, :, pl.ds(layout.offset + 2 * half * rows, 2 * rows)]
                loads.append(self.load(part, held.at[:, :, pl.ds(2 * half * rows, 2 * rows)]))
            return loads
        start = self.count
        self.count += 8
        for dp in range(2):

            @pl.when(place[2] == dp)
            def _():
                for copy in self.piece_copies(place, pieces, layout, held, dp, start):
                    copy.start()

        copies = list(self.piece_copies(place, pieces, layout, held, 0, start))
        return [Loaded(held, copies[:4]), Loaded(held, copies[4:])]

    def piece_copies(self, place, pieces, layout, held, dp, sem):
        rows = held.shape[2] // 4
        for half in range(2):
            for turn in range(2):
                for first in range(2):
                    y, which = place[1] ^ first, place[3] ^ turn
                    quarter = pl.multiple_of((2 * half + which) * rows, rows)
                    piece = pieces[4 * turn + 2 * first + (half ^ dp)]
                    yield pltpu.make_async_copy(
                        piece.at[:, :, pl.ds(layout.offset, rows)],
                        held.at[:, pl.ds(2 * y, 2), pl.ds(quarter, rows)],
                        self.sems.at[sem],
                    )
                    sem += 1

    def deliver(self, place, held, layout, outs, *quarters):
        rows = held.shape[2] // 4
        if layout.made == 1:
            for quarter in (q for q in quarters if q < 4):
                part = pl.ds(layout.made_offset + quarter * rows, rows)
                self.store(held.at[:, :, pl.ds(quarter * rows, rows)], outs[0].at[:, :, part])
        elif 4 in quarters:
            for turn in range(2):
                for first in range(2):
                    for second in range(2):
                        y, half, which = place_of(place, turn, first, second)
                        quarter = pl.multiple_of((2 * half + which) * rows, rows)
                        self.store(
                            held.at[:, pl.ds(2 * y, 2), pl.ds(quarter, rows)],
                            outs[turn].at[first, second],
                        )


def place_of(place, turn, first, second):
    which = place[3] ^ turn
    y = place[1] ^ jnp.where(which == 0, first, second)
    half = place[2] ^ jnp.where(which == 0, second, first)
    return y, half, which


class Loaded:
    def __init__(self, target, copies):
        self.target, self.copies = target, copies

    def arrive(self):
        wait_all(self.copies)
        self.copies.clear()
        return self.target

    def __getitem__(self, index):
        return self.arrive()[index]


def self_forward_part(copies, row, gains, bias, inputs, loads, held, scratch, outs):
    out, normed, joined, probs, mixed = scratch
    out_ref, normed_ref, joined_ref, probs_ref, mixed_ref = outs
    passes = len(inputs)
    for p in range(passes):
        rows = slice(p * TOK, (p + 1) * TOK)
        unit, unused = normed_of(inputs[p][...].astype(F32))
        normed[rows] = (unit * gains[row : row + 1] + gains[row + 1 : row + 2]).astype(BF)
    copies.store(normed, normed_ref)
    for b in range(3):
        loads[b // 2].arrive()
        joined[:, b * D : (b + 1) * D] = dot(normed[...], column_block(held, b)).astype(BF)
    copies.store(joined, joined_ref)
    for p in range(passes):
        rows = slice(p * TOK, (p + 1) * TOK)
        mixed_part = attend(
            joined[rows, 0:D], joined[rows, D : 2 * D], joined[rows, 2 * D : 3 * D], bias, probs, p * HEADS
        )
        heads = pl.ds(p * HEADS, HEADS)
        copies.store(probs.at[heads], probs_ref.at[heads])
        mixed[rows] = mixed_part
        out[rows] = inputs[p][...].astype(F32) + dot(mixed_part, column_block(held, 3))
    copies.store(out, out_ref)
    copies.store(mixed, mixed_ref)


def norm_table(copies, place, pieces, gains, held):
    loads = [
        copies.load(pieces[2 * k].at[:, :, pl.ds(64, 16)], held.at[k]) for k in range(2)
    ]

    def compute():
        for load in loads:
            load.arrive()
        for y in range(2):
            where = jnp.where(place[1] == y, 0, 1)
            for z in range(4):
                for core in range(2):
                    spot = 4 * z + 2 * y + core
                    row = held[where, z, core]
                    gains[:, spot * BLOCK : (spot + 1) * BLOCK] = row[:, 0:BLOCK].astype(F32)

    return compute


def self_forward_kernel(decoder, encoder, me_ref, src_lengths, tgt_lengths, given, *refs):
    taken, refs = refs[:3], refs[3:]
    pieces, refs = refs[: decoder.pieces], refs[decoder.pieces :]
    more, refs = refs[: encoder.pieces], refs[encoder.pieces :]
    outs, gains, scratch, (held, held_enc, held_norm, *come, sems) = refs[:10], refs[10], refs[11:21], refs[21:]
    copies = Copies(sems)
    table = norm_table(copies, me_ref, pieces, gains, held_norm) if decoder.pieces > 1 else None
    inputs = [copies.load(taken[p], come[p]) for p in range(3)]
    loads = copies.fetch(me_ref, pieces, decoder, held)
    loads_enc = copies.fetch(me_ref, more, encoder, held_enc)
    bias = mask_bias(tgt_lengths, tgt_lengths)
    if table:
        table()
    else:
        gains[...] = given[...]
    self_forward_part(copies, 4, gains, bias, inputs[:2], loads, held, scratch[:5], outs[:5])
    bias = mask_bias(src_lengths, src_lengths)
    self_forward_part(copies, 0, gains, bias, inputs[2:], loads_enc, held_enc, scratch[5:], outs[5:])
    copies.finish()


def self_back_kernel(passes, row, more, layout, me_ref, gains, *refs):
    others, refs = refs[:more], refs[more:]
    inputs, refs = refs[:passes], refs[passes:]
    taken, refs = refs[:5], refs[5:]
    pieces, refs = refs[: layout.pieces], refs[layout.pieces :]
    grad_in_ref, norm_ref, *refs = refs
    outs, refs = refs[: layout.made], refs[layout.made :]
    grad_in, held, made, back, grad_out, normed, joined, probs, mixed, *come, sems = refs
    copies = Copies(sems)
    grad_out = copies.load(taken[0], grad_out)
    mixed = copies.load(taken[4], mixed)
    loads = copies.fetch(me_ref, pieces, layout, held)
    probs = [
        copies.load(taken[3].at[pl.ds(p * HEADS, HEADS)], probs.at[pl.ds(p * HEADS, HEADS)])
        for p in range(passes)
    ]
    joined = copies.load(taken[2], joined)
    normed = copies.load(taken[1], normed)
    inputs = [copies.load(inputs[p], come[p]) for p in range(passes)]
    grad_low = grad_out[...].astype(BF)
    put_block(made, 3, dot_tn(mixed[...], grad_low))
    copies.deliver(me_ref, made, layout, outs, 3)
    loads[1].arrive()
    grad_mixed = dot_nt(grad_low, column_block(held, 3)).astype(BF)
    for p in range(passes):
        rows = slice(p * TOK, (p + 1) * TOK)
        grads = attend_back(
            joined[rows, 0:D],
            joined[rows, D : 2 * D],
            joined[rows, 2 * D : 3 * D],
            probs[p].arrive(),
            0,
            grad_mixed[rows],
        )
        for b in range(3):
            back[rows, b * D : (b + 1) * D] = grads[b].astype(BF)
    loads[0].arrive()
    for b in range(3):
        part = back[:, b * D : (b + 1) * D]
        put_block(made, b, dot_tn(normed[...], part))
        copies.deliver(me_ref, made, layout, outs, b)
    copies.deliver(me_ref, made, layout, outs, 4)
    grad_normed = None
    for b in range(3):
        step = dot_nt(back[:, b * D : (b + 1) * D], column_block(held, b))
        grad_normed = step if grad_normed is None else grad_normed + step
    units = [normed_of(inputs[p][...].astype(F32)) for p in range(passes)]
    unit = jnp.concatenate([u[0] for u in units], axis=0)
    inverse = jnp.concatenate([u[1] for u in units], axis=0)
    if more:
        norm_ref[...] = jnp.zeros(norm_ref.shape, F32)
        for k, other in enumerate(others):
            norm_ref[2 * k + 2 : 2 * k + 4] = other[...]
    grad = norm_back(unit, inverse, gains[row : row + 1], grad_normed, norm_ref)
    grad_in[...] = grad_out[0:TOK] + grad[0:TOK]
    copies.store(grad_in, grad_in_ref)
    copies.finish()


GELU_SCALE = 0.7978845608028654
GELU_CUBE = 0.044715


def gelu_both(up):
    square = up * up
    bent = jnp.tanh(up * (GELU_SCALE + (GELU_SCALE * GELU_CUBE) * square))
    half = 0.5 + 0.5 * bent
    inner = 2.0 * GELU_SCALE + (6.0 * GELU_SCALE * GELU_CUBE) * square
    return up * half, half + up * (half - half * half) * inner


def ffn_grads(copies, place, layout, outs, gain, hidden, grad_low, normed, active, slope, norm_ref, held, made):
    for z in range(4):
        product = dot_tn(active[:, z * D : (z + 1) * D], grad_low)
        made[z, :, 4 * BLOCK : 8 * BLOCK] = product.astype(BF).reshape(4, 4 * BLOCK, D)
    copies.deliver(place, made, layout, outs, 2)
    copies.deliver(place, made, layout, outs, 3)
    grad_normed = None
    for b in range(4):
        cols = slice(b * D, (b + 1) * D)
        grad_active = dot_nt(grad_low, row_block(held, b))
        grad_up = (slope[:, cols].astype(F32) * grad_active).astype(BF)
        put_block(made, b, dot_tn(normed[...], grad_up))
        if b % 2 == 1:
            copies.deliver(place, made, layout, outs, b // 2)
        step = dot_nt(grad_up, column_block(held, b))
        grad_normed = step if grad_normed is None else grad_normed + step
    copies.deliver(place, made, layout, outs, 4)
    unit, inverse = normed_of(hidden)
    return norm_back(unit, inverse, gain, grad_normed, norm_ref)


def ffn_back_kernel(row, layout, me_ref, gains, *refs):
    taken, refs = refs[:5], refs[5:]
    pieces, refs = refs[: layout.pieces], refs[layout.pieces :]
    grad_in_ref, norm_ref, *refs = refs
    outs, refs = refs[: layout.made], refs[layout.made :]
    grad_in, held, made, hidden, grad_out, normed, active, slope, sems = refs
    copies = Copies(sems)
    grad_out = copies.load(taken[1], grad_out)
    active = copies.load(taken[3], active)
    loads = copies.fetch(me_ref, pieces, layout, held)
    slope = copies.load(taken[4], slope)
    normed = copies.load(taken[2], normed)
    hidden = copies.load(taken[0], hidden)
    grad_low = grad_out[...].astype(BF)
    active = active.arrive()
    for load in loads:
        load.arrive()
    hidden.arrive()
    grad = ffn_grads(
        copies, me_ref, layout, outs, gains[row : row + 1], hidden[...], grad_low, normed, active, slope, norm_ref, held, made
    )
    grad_in[...] = grad_out[...] + grad
    copies.store(grad_in, grad_in_ref)
    copies.finish()


def second_kernel(encoder, cross, me_ref, src_lengths, tgt_lengths, gains, *refs):
    taken, whole, refs = refs[:2], refs[2:4], refs[4:]
    sent, made, (held_enc, held_cross, hidden_enc, hidden_one, sems) = refs[:10], refs[10:20], refs[20:]
    normed_enc, active_enc, slope_enc, memory, normed, query, pair, probs, mixed, hidden = made
    copies = Copies(sems)
    hidden_enc = copies.load(taken[0], hidden_enc)
    loads_enc = copies.fetch(me_ref, whole[:1], encoder, held_enc)
    hidden_one = copies.load(taken[1], hidden_one)
    loads_cross = copies.fetch(me_ref, whole[1:], cross, held_cross)

    unit, unused = normed_of(hidden_enc[...])
    normed_enc[...] = (unit * gains[2:3] + gains[3:4]).astype(BF)
    copies.store(normed_enc, sent[0])
    unit, unused = normed_of(hidden_one[...])
    normed[...] = (unit * gains[6:7] + gains[7:8]).astype(BF)
    copies.store(normed, sent[4])
    loads_enc[0].arrive()
    for b in range(4):
        cols = slice(b * D, (b + 1) * D)
        grown, bent = gelu_both(dot(normed_enc[...], column_block(held_enc, b)))
        active_enc[:, cols] = grown.astype(BF)
        slope_enc[:, cols] = bent.astype(BF)
    copies.store(active_enc, sent[1])
    copies.store(slope_enc, sent[2])
    loads_enc[1].arrive()
    total = hidden_enc[...]
    for z in range(4):
        total = total + dot(active_enc[:, z * D : (z + 1) * D], row_block(held_enc, z))
    memory[...] = total.astype(BF)
    copies.store(memory, sent[3])

    loads_cross[0].arrive()
    query[...] = dot(normed[...], column_block(held_cross, 0)).astype(BF)
    copies.store(query, sent[5])
    pair[:, 0:D] = dot(memory[...], column_block(held_cross, 1)).astype(BF)
    loads_cross[1].arrive()
    pair[:, D : 2 * D] = dot(memory[...], column_block(held_cross, 2)).astype(BF)
    copies.store(pair, sent[6])
    bias = mask_bias(src_lengths, tgt_lengths)
    for p in range(2):
        rows = slice(p * TOK, (p + 1) * TOK)
        part = attend(query[rows], pair[:, 0:D], pair[:, D : 2 * D], bias, probs, p * HEADS)
        heads = pl.ds(p * HEADS, HEADS)
        copies.store(probs.at[heads], sent[7].at[heads])
        mixed[rows] = part
        hidden[rows] = hidden_one[rows] + dot(part, column_block(held_cross, 3))
    copies.store(mixed, sent[8])
    copies.store(hidden, sent[9])
    copies.finish()


def middle_kernel(cross, decoder, me_ref, gains, *refs):
    taken, whole, refs = refs[:10], refs[10:11], refs[11:]
    pieces, refs = refs[: decoder.pieces], refs[decoder.pieces :]
    norm_ffn, norm_cross, *refs = refs
    sent, refs = refs[:5], refs[5:]
    come, refs = refs[:10], refs[10:]
    held_cross, held, made_cross, made, first_out, second_out, grad_memory, grad_one, *refs = refs
    normed_two, active, slope, grad_two, back, sems = refs
    copies = Copies(sems)
    hidden = copies.load(taken[0], come[0])
    loads = copies.fetch(me_ref, pieces, decoder, held)
    cots = [copies.load(taken[k], come[k]) for k in (1, 2)]
    loads_cross = copies.fetch(me_ref, whole, cross, held_cross)
    mixed, probs, query, pair, normed, memory, hidden_one = (
        copies.load(taken[k], come[k]) for k in range(3, 10)
    )

    unit, unused = normed_of(hidden[...])
    normed_two[...] = (unit * gains[8:9] + gains[9:10]).astype(BF)
    loads[0].arrive()
    for b in range(4):
        cols = slice(b * D, (b + 1) * D)
        grown, bent = gelu_both(dot(normed_two[...], column_block(held, b)))
        active[:, cols] = grown.astype(BF)
        slope[:, cols] = bent.astype(BF)
    loads[1].arrive()
    total = hidden[...]
    for z in range(4):
        total = total + dot(active[:, z * D : (z + 1) * D], row_block(held, z))
    first_out[...] = total[0:TOK].astype(BF)
    second_out[...] = total[TOK:].astype(BF)
    copies.store(first_out, sent[0])
    copies.store(second_out, sent[1])
    grad_low = jnp.concatenate([cots[0][...], cots[1][...]], axis=0)
    grad = ffn_grads(
        copies, me_ref, decoder, sent[4:], gains[8:9], hidden[...], grad_low, normed_two, active, slope, norm_ffn, held, made
    )
    grad_two[...] = grad_low.astype(F32) + grad

    grad_low = grad_two[...].astype(BF)
    put_block(made_cross, 3, dot_tn(mixed[...], grad_low))
    copies.deliver(me_ref, made_cross, cross, sent[4:], 3)
    loads_cross[1].arrive()
    grad_mixed = dot_nt(grad_low, column_block(held_cross, 3)).astype(BF)
    grad_key = grad_value = None
    probs = probs.arrive()
    for p in range(2):
        rows = slice(p * TOK, (p + 1) * TOK)
        grads = attend_back(
            query[rows], pair[:, 0:D], pair[:, D : 2 * D], probs, p * HEADS, grad_mixed[rows]
        )
        back[rows] = grads[0].astype(BF)
        grad_key = grads[1] if grad_key is None else grad_key + grads[1]
        grad_value = grads[2] if grad_value is None else grad_value + grads[2]
    grad_key = grad_key.astype(BF)
    grad_value = grad_value.astype(BF)
    for b, (left, right) in enumerate(
        ((normed[...], back[...]), (memory[...], grad_key), (memory[...], grad_value))
    ):
        put_block(made_cross, b, dot_tn(left, right))
        copies.deliver(me_ref, made_cross, cross, sent[4:], b)
    loads_cross[0].arrive()
    grad_memory[...] = dot_nt(grad_key, column_block(held_cross, 1)) + dot_nt(
        grad_value, column_block(held_cross, 2)
    )
    copies.store(grad_memory, sent[2])
    grad_normed = dot_nt(back[...], column_block(held_cross, 0))
    unit, inverse = normed_of(hidden_one[...])
    grad = norm_back(unit, inverse, gains[6:7], grad_normed, norm_cross)
    grad_one[...] = grad_two[...] + grad
    copies.store(grad_one, sent[3])
    copies.finish()


ANY = pl.BlockSpec(memory_space=pl.ANY)
HB = pl.BlockSpec(memory_space=pltpu.HBM)
VM = pl.BlockSpec(memory_space=pltpu.VMEM)
SM = pl.BlockSpec(memory_space=pltpu.SMEM)


def held_of(blocks):
    return pltpu.VMEM((4, 4, blocks * BLOCK, D), BF)


def made_of(layout, blocks):
    if layout.made == 1:
        return [jax.ShapeDtypeStruct((4, 4, layout.made_rows, D), BF)]
    return [jax.ShapeDtypeStruct((2, 2, 4, 2, blocks * BLOCK // 4, D), BF)] * 2


def shape(rows, cols, dtype):
    return jax.ShapeDtypeStruct((rows, cols), dtype)


class Order:
    def __init__(self):
        self.token = None

    def tie(self, value):
        return self.tie_all([value])[0]

    def tie_all(self, values):
        arrays = list(values) + [self.token]
        *values, self.token = pl.pallas_call(
            nothing_kernel,
            name="tie",
            out_shape=[jax.ShapeDtypeStruct(x.shape, x.dtype) for x in arrays],
            in_specs=[HB] * len(arrays),
            out_specs=[HB] * len(arrays),
            input_output_aliases={k: k for k in range(len(arrays))},
            compiler_params=pltpu.CompilerParams(vmem_limit_bytes=VMEM_LIMIT),
        )(*arrays)
        return values


def nothing_kernel(*refs):
    pass


def call(order, body, name, in_specs, out_shape, out_specs, scratch, operands, micros, grid=None, inplace=()):
    inplace = list(inplace) + ([(order.token, len(out_shape))] if order.token is not None else [])
    count, more, outs = len(operands), len(inplace), len(out_shape)

    def ordered(*refs):
        body(*refs[:count], *refs[count + more : count + more + outs], *refs[count + more + outs + 1 :])

    aliases = {count + k: out for k, (unused, out) in enumerate(inplace)}
    *results, order.token = pl.pallas_call(
        ordered,
        name=name,
        out_shape=out_shape + [jax.ShapeDtypeStruct((8, 128), F32)],
        in_specs=in_specs + [HB] * more,
        out_specs=out_specs + [HB],
        input_output_aliases=aliases,
        scratch_shapes=scratch,
        compiler_params=pltpu.CompilerParams(vmem_limit_bytes=VMEM_LIMIT),
        cost_estimate=pl.CostEstimate(
            flops=int((micros + 0.01) * COST), bytes_accessed=0, transcendentals=0
        ),
        **({} if grid is None else {"grid": grid}),
    )(*operands, *(array for array, unused in inplace))
    return results


def vmem(rows, cols, dtype):
    return pltpu.VMEM((rows, cols), dtype)


def probs_of(count, scratch=False):
    dims = (count * HEADS, TOK, TOK)
    return pltpu.VMEM(dims, BF) if scratch else jax.ShapeDtypeStruct(dims, BF)


SEMS = pltpu.SemaphoreType.DMA((64,))


def arrays(items):
    return [jax.ShapeDtypeStruct(dims, dtype) for dims, dtype in items]


def buffers(items):
    return [pltpu.VMEM(dims, dtype) for dims, dtype in items]


def self_kept(count):
    rows = count * TOK
    return [
        ((rows, D), F32),
        ((rows, D), BF),
        ((rows, 3 * D), BF),
        ((count * HEADS, TOK, TOK), BF),
        ((rows, D), BF),
    ]


def self_forward(order, me, src_lengths, tgt_lengths, gains, inputs, decoder, encoder):
    kept = self_kept(2) + self_kept(1)
    results = call(
        order,
        functools.partial(self_forward_kernel, decoder[0], encoder[0]),
        "self_forward",
        [SM, SM, SM, ANY if decoder[0].pieces > 1 else VM] + [HB] * 3 + [ANY] * (decoder[0].pieces + encoder[0].pieces),
        arrays(kept) + [shape(16, D, F32)],
        [HB] * 10 + [VM],
        buffers(kept)
        + [held_of(4), held_of(4), pltpu.VMEM((2, 4, 2, 16, D), BF)]
        + [vmem(TOK, D, BF)] * 3
        + [SEMS],
        (me, src_lengths, tgt_lengths, gains, *inputs, *decoder[1], *encoder[1]),
        12,
    )
    return results[:5], results[5:10], results[10]


def second(order, me, src_lengths, tgt_lengths, gains, hidden_enc, hidden_one, encoder, cross):
    rows = 2 * TOK
    kept = [
        ((TOK, D), BF),
        ((TOK, FF), BF),
        ((TOK, FF), BF),
        ((TOK, D), BF),
        ((rows, D), BF),
        ((rows, D), BF),
        ((TOK, 2 * D), BF),
        ((2 * HEADS, TOK, TOK), BF),
        ((rows, D), BF),
        ((rows, D), F32),
    ]
    results = call(
        order,
        functools.partial(second_kernel, encoder[0], cross[0]),
        "second",
        [SM, SM, SM, VM] + [HB] * 2 + [ANY] * 2,
        arrays(kept),
        [HB] * 10,
        buffers(kept) + [held_of(8), held_of(4), vmem(TOK, D, F32), vmem(rows, D, F32), SEMS],
        (me, src_lengths, tgt_lengths, gains, hidden_enc, hidden_one, encoder[1][0], cross[1][0]),
        13,
    )
    return results[:3], results[3:]


def self_back(order, row, me, gains, inputs, grad_out, kept, pieces, others=()):
    count = len(inputs)
    rows = count * TOK
    return call(
        order,
        functools.partial(self_back_kernel, count, row, len(others), pieces[0]),
        "self_back",
        [SM, VM] + [VM] * len(others) + [HB] * count + [HB] * 5 + [ANY] * pieces[0].pieces,
        [shape(TOK, D, F32), shape(16 if others else 2, D, F32)] + made_of(pieces[0], 4),
        [HB, VM] + [HB] * pieces[0].made,
        [
            vmem(TOK, D, F32),
            held_of(4),
            held_of(4),
            vmem(rows, 3 * D, BF),
            vmem(rows, D, F32),
            vmem(rows, D, BF),
            vmem(rows, 3 * D, BF),
            probs_of(count, True),
            vmem(rows, D, BF),
        ]
        + [vmem(TOK, D, BF)] * count
        + [SEMS],
        (me, gains, *others, *inputs, grad_out, *kept, *pieces[1]),
        5.8 + 3.4 * count,
    )


def ffn_back(order, row, me, gains, hidden, grad_out, kept, pieces):
    return call(
        order,
        functools.partial(ffn_back_kernel, row, pieces[0]),
        "ffn_back",
        [SM, VM] + [HB] * 5 + [ANY] * pieces[0].pieces,
        [shape(TOK, D, F32), shape(2, D, F32)] + made_of(pieces[0], 8),
        [HB, VM] + [HB] * pieces[0].made,
        [
            vmem(TOK, D, F32),
            held_of(8),
            held_of(8),
            vmem(TOK, D, F32),
            vmem(TOK, D, F32),
            vmem(TOK, D, BF),
            vmem(TOK, FF, BF),
            vmem(TOK, FF, BF),
            SEMS,
        ],
        (me, gains, hidden, grad_out, *kept, *pieces[1]),
        10.2,
    )


def middle(order, me, gains, hidden_one, kept, cots, cross, decoder):
    rows = 2 * TOK
    memory, normed, query, pair, probs, mixed, hidden = kept
    taken = [hidden, *cots, mixed, probs, query, pair, normed, memory, hidden_one]
    sent = [((TOK, D), BF), ((TOK, D), BF), ((TOK, D), F32), ((rows, D), F32)]
    return call(
        order,
        functools.partial(middle_kernel, cross[0], decoder[0]),
        "middle",
        [SM, VM] + [HB] * 10 + [ANY] * (1 + decoder[0].pieces),
        [shape(2, D, F32)] * 2 + arrays(sent + [((4, 4, 384, D), BF)]),
        [VM] * 2 + [HB] * 5,
        buffers([(x.shape, x.dtype) for x in taken])
        + [held_of(4), held_of(8), held_of(4), held_of(8)]
        + buffers(sent)
        + [
            vmem(rows, D, BF),
            vmem(rows, FF, BF),
            vmem(rows, FF, BF),
            vmem(rows, D, F32),
            vmem(rows, D, BF),
            SEMS,
        ],
        (me, gains, *taken, cross[1][0], *decoder[1]),
        25,
    )


AXIS = "fsdp"
BOTH = ("dp", "fsdp")
SHARDS = 16


def route(target):
    pairs = []
    for i in range(2 * SHARDS):
        dp, z, y, core = target(i // 16, (i // 4) % 4, (i // 2) % 2, i % 2)
        pairs.append((i, dp * 16 + (z % 4) * 4 + y * 2 + core))
    return pairs


def to_core(x):
    return lax.ppermute(x, BOTH, route(lambda dp, z, y, core: (dp, z, y, 1 - core)))


def to_z(x, step):
    return lax.ppermute(x, BOTH, route(lambda dp, z, y, core: (dp, z + step, y, core)))


def to_z_pair(x, step):
    return lax.ppermute(x, BOTH, route(lambda dp, z, y, core: (dp, z ^ step, y, core)))


def to_y(x):
    return lax.ppermute(x, BOTH, route(lambda dp, z, y, core: (dp, z, 1 - y, core)))


def to_dp(x):
    return lax.ppermute(x, BOTH, route(lambda dp, z, y, core: (1 - dp, z, y, core)))


def to_yx(x):
    return lax.ppermute(
        x, BOTH, route(lambda dp, z, y, core: (dp, z, y ^ 1, core) if core == 0 else (dp ^ 1, z, y, core))
    )


def to_xy(x):
    return lax.ppermute(
        x, BOTH, route(lambda dp, z, y, core: (dp ^ 1, z, y, core) if core == 0 else (dp, z, y ^ 1, core))
    )


def blocks_of(shard):
    rows, cols = shard.shape
    split = shard.reshape(rows // BLOCK, BLOCK, cols // D, D)
    return split.transpose(2, 0, 1, 3).reshape(-1, BLOCK, D)


def shard_of(blocks, cols):
    wide = blocks.reshape(cols // D, -1, D)
    return wide.transpose(1, 0, 2).reshape(-1, cols)


def small(order, body, name, out, operands, scratch=(), in_specs=None, out_specs=None, micros=0, grid=None):
    return call(
        order,
        body,
        name,
        in_specs if in_specs is not None else [VM] * len(operands),
        [jax.ShapeDtypeStruct(dims, dtype) for dims, dtype in out],
        out_specs if out_specs is not None else [VM] * len(out),
        list(scratch),
        operands,
        micros,
        grid,
    )


def pack_kernel(*refs):
    weights, (one, two, three, place, norms) = refs[:15], refs[15:]
    spot = lax.axis_index(AXIS)
    place[0] = spot >> 2
    place[1] = (spot >> 1) & 1
    place[2] = lax.axis_index("dp")
    place[3] = spot & 1
    self_in, self_out, enc_in, enc_out, enc_ffn_in, enc_ffn_out = weights[:6]
    cross_q, cross_kv, cross_out, ffn_in, ffn_out = weights[6:11]
    for half in range(2):

        @pl.when(place[2] == half)
        def _():
            for k in range(2):
                quarter = 2 * half + k
                cols = slice(quarter * D, (quarter + 1) * D)
                one[k, 0:32] = self_out[...] if quarter == 3 else self_in[:, cols]
                one[k, 32:64] = enc_out[...] if quarter == 3 else enc_in[:, cols]
                for j in range(2):
                    block = 2 * quarter + j
                    rows = slice(j * BLOCK, (j + 1) * BLOCK)
                    cols = slice(block * D, (block + 1) * D)
                    part = slice((block - 4) * BLOCK, (block - 3) * BLOCK)
                    three[k, rows] = ffn_in[:, cols] if block < 4 else ffn_out[part]

    for block in range(4):
        rows = slice(block * BLOCK, (block + 1) * BLOCK)
        two[rows] = enc_ffn_in[:, block * D : (block + 1) * D]
    two[128:256] = enc_ffn_out[...]
    two[256:288] = cross_q[...]
    two[288:320] = cross_kv[:, 0:D]
    two[320:352] = cross_kv[:, D : 2 * D]
    two[352:384] = cross_out[...]
    norms[...] = jnp.zeros(norms.shape, F32)
    row = 0
    for gain, bias in (weights[11:13], weights[13:15]):
        for k in range(gain.shape[0]):
            norms[row : row + 1, 0:BLOCK] = gain[k : k + 1].astype(F32)
            norms[row + 1 : row + 2, 0:BLOCK] = bias[k : k + 1].astype(F32)
            row += 2
    for k in range(2):
        one[k, 64:80] = norms[...].astype(BF)


def pack(order, weights, norms):
    return small(
        order,
        pack_kernel,
        "pack",
        [((2, 80, D), BF), ((384, D), BF), ((2, 64, D), BF), ((4,), jnp.int32)],
        (*weights, *norms),
        [pltpu.VMEM((16, D), F32)],
        in_specs=[VM] * 15,
        out_specs=[VM] * 3 + [SM],
    )


def pair_kernel(place, *refs):
    core = place[3]
    for k in range(2):
        mine, near, pair = refs[2 * k], refs[2 * k + 1], refs[4 + k]
        pair[core] = mine[core]
        pair[1 - core] = near[core]


def pair_up(order, place, mine, near):
    operands = [x for both in zip(mine, near) for x in both]
    return small(
        order,
        pair_kernel,
        "pair_up",
        [(x.shape, x.dtype) for x in mine],
        (place, *operands),
        in_specs=[SM] + [VM] * 4,
    )


def stack_kernel(place, *refs):
    parts, (out, held, sems) = refs[:-3], refs[-3:]
    count = len(parts)
    loads = [pltpu.make_async_copy(parts[d], held.at[d], sems.at[d]) for d in range(count)]
    stores = [
        pltpu.make_async_copy(held.at[d], out.at[(place[0] + (4 - d)) & 3], sems.at[count + d])
        for d in range(count)
    ]
    for copy in loads:
        copy.start()
    for d in range(count):
        loads[d].wait()
        stores[d].start()
    wait_all(stores)


def stack(order, place, parts):
    dims = (len(parts),) + parts[0].shape
    dtype = parts[0].dtype
    return small(
        order,
        stack_kernel,
        "stack",
        [(dims, dtype)],
        (place, *parts),
        [pltpu.VMEM(dims, dtype), pltpu.SemaphoreType.DMA((2 * len(parts),))],
        [SM] + [ANY] * len(parts),
        [ANY],
    )[0]


class Gather:
    def __init__(self, order, pair):
        self.order, self.pair = order, pair

    def along_z(self):
        pair = self.order.tie(self.pair)
        self.parts = [pair] + [to_z(pair, d) for d in (1, 2, 3)]

    def lined(self, place):
        self.line = stack(self.order, place, self.parts)

    def first_cross(self):
        line = self.order.tie(self.line)
        self.own = [line, to_dp(line), to_y(line)]
        self.near = []

    def crossed(self, others=()):
        arrived = self.order.tie_all(self.own[1:3] + list(others[1:]))
        self.own[1:3] = arrived[:2]
        if others:
            others[1:] = arrived[2:]

    def second_cross(self):
        self.own.append(to_dp(self.own[2]))

    def share(self):
        self.near = [to_core(piece) for piece in self.own[:3]]

    def done(self):
        last, *self.near = self.order.tie_all([self.own[3]] + self.near)
        self.own = self.own[:3] + [last]
        self.near.append(self.order.tie(to_core(last)))
        self.pieces = tuple(self.own + self.near)


def low_sum(*parts):
    total = parts[0].astype(F32)
    for part in parts[1:]:
        total = total + part.astype(F32)
    return total.astype(BF)


def rows_of(parts):
    row = 0
    for k, part in enumerate(parts[::2]):
        yield slice(row, row + part.shape[4]), part, parts[2 * k + 1]
        row += part.shape[4]


def send_block(step, source, target, sems, more):
    def copies():
        for k in range(4):
            yield k, pltpu.make_async_copy(
                source.at[k], target.at[pl.ds(k * source.shape[1], source.shape[1])], sems.at[k]
            )

    last = pltpu.make_async_copy(*more, sems.at[4])
    for k, copy in copies():
        pl.when(step == k)(copy.start)
    pl.when(step == 0)(last.start)

    @pl.when(step == 3)
    def _():
        for unused, copy in copies():
            copy.wait()
        last.wait()


def reduce_first_kernel(norm_own, norm_came, *refs):
    sent, held, norm, sems = refs[-4:]
    step = pl.program_id(0)

    @pl.when(step == 0)
    def _():
        norm[...] = (norm_own[...] + norm_came[...]).astype(BF)

    whole = held.shape[1] // 4
    for rows, own, came in rows_of(refs[:-4]):
        for second in range(2):
            for core in range(2):
                row = (2 * second + core) * whole + rows.start
                held[step, row : row + rows.stop - rows.start] = (
                    own[0, second, 0, core] + came[0, second, 0, core]
                )
    send_block(step, held, sent, sems, (norm, sent.at[pl.ds(16 * whole, 16)]))


def reduce_second_kernel(norm_own, norm_came, came_first, *refs):
    sent, held, norm, sems = refs[-4:]
    step = pl.program_id(0)

    @pl.when(step == 0)
    def _():
        norm[...] = (norm_own[...].astype(F32) + norm_came[...].astype(F32)).astype(BF)

    whole = held.shape[1] // 2
    for rows, own, came in rows_of(refs[:-4]):
        for core in range(2):
            span = slice(core * whole + rows.start, core * whole + rows.stop)
            held[step, span] = low_sum(own[0, 0, 0, core], came[0, 0, 0, core], came_first[span])
    send_block(step, held, sent, sems, (norm, sent.at[pl.ds(8 * whole, 16)]))


def reduce_third_kernel(norm_own, norm_came, place, came_first, came_second, *refs):
    outs = refs[-4:]
    norm = (norm_own[...].astype(F32) + norm_came[...].astype(F32)).astype(BF)
    whole = (outs[0].shape[0] - 16) // 2
    for d in range(4):
        z = (place[0] + d) & 3
        outs[d][2 * whole :] = norm
        for rows, own, came in rows_of(refs[:-4]):
            for core in range(2):
                span = slice(core * whole + rows.start, core * whole + rows.stop)
                size = rows.stop - rows.start
                first = pl.multiple_of(z * 4 * whole + span.start, 16)
                second = pl.multiple_of(z * 2 * whole + span.start, 16)
                outs[d][span] = low_sum(
                    own[0, 0, z, core],
                    came[0, 0, z, core],
                    came_first[pl.ds(first, size)],
                    came_second[pl.ds(second, size)],
                )


def reduce_fourth_kernel(a, b, c, d, out, norm):
    rows = out.shape[1]
    for core in range(2):
        span = slice(core * rows, (core + 1) * rows)
        out[core] = low_sum(a[span], b[span], c[span], d[span])
    total = a[2 * rows :].astype(F32)
    for part in (b, c, d):
        total = total + part[2 * rows :].astype(F32)
    norm[...] = total


class Reduce:
    def __init__(self, order):
        self.order, self.own, self.came = order, [], []

    def add(self, own, other):
        self.own.append(own)
        self.came.append(to_core(self.order.tie(other)))

    def arrive(self):
        self.came[-1] = self.order.tie(self.came[-1])

    def start_norm(self, norm):
        self.norm = self.order.tie(norm)
        self.norm_came = to_core(self.norm)

    def run(self, body, name, dims, operands, in_specs, part_spec, out_specs=None, scratch=(), grid=(4,)):
        parts = [x for both in zip(self.own, self.came) for x in both]
        specs = [pl.BlockSpec(part_spec[0] + (part.shape[4], D), part_spec[1]) for part in parts]
        sent = small(
            self.order,
            body,
            name,
            [(item, BF) for item in dims],
            operands + parts,
            scratch,
            in_specs=in_specs + specs,
            out_specs=out_specs or [HB] * len(dims),
            grid=grid,
        )
        return [self.order.tie(x) for x in sent]

    def first(self):
        rows = self.rows = sum(own.shape[4] for own in self.own)
        norm_spec = pl.BlockSpec((16, D), lambda i: (0, 0))
        (self.first_sent,) = self.run(
            reduce_first_kernel,
            "reduce_first",
            [(16 * rows + 16, D)],
            [self.norm, self.norm_came],
            [norm_spec] * 2,
            ((1, 2, 1, 2), lambda i: (1, 0, i, 0, 0, 0)),
            scratch=buffers([((4, 4 * rows, D), BF), ((16, D), BF)]) + [pltpu.SemaphoreType.DMA((5,))],
        )
        self.first_came = to_yx(self.first_sent)

    def second(self):
        rows = self.rows
        norm_spec = pl.BlockSpec((16, D), lambda i: (rows, 0))
        (self.second_sent,) = self.run(
            reduce_second_kernel,
            "reduce_second",
            [(8 * rows + 16, D)],
            [self.first_sent, self.first_came, self.first_came],
            [norm_spec] * 2 + [pl.BlockSpec((2 * rows, D), lambda i: (2 * i + 1, 0))],
            ((1, 1, 1, 2), lambda i: (0, 1, i, 0, 0, 0)),
            scratch=buffers([((4, 2 * rows, D), BF), ((16, D), BF)]) + [pltpu.SemaphoreType.DMA((5,))],
        )
        self.second_came = to_xy(self.second_sent)

    def third(self, place):
        rows = self.rows
        norm_spec = pl.BlockSpec((16, D), lambda i: (rows // 2, 0))
        parts = self.run(
            reduce_third_kernel,
            "reduce_third",
            [(2 * rows + 16, D)] * 4,
            [self.second_sent, self.second_came, place, self.first_came, self.second_came],
            [norm_spec] * 2
            + [SM]
            + [pl.BlockSpec(x.shape, lambda i: (0, 0)) for x in (self.first_came, self.second_came)],
            ((1, 1, 4, 2), lambda i: (0, 0, 0, 0, 0, 0)),
            [pl.BlockSpec((2 * rows + 16, D), lambda i: (0, 0))] * 4,
            grid=(1,),
        )
        self.lines = [parts[0]] + [to_z(parts[d], d) for d in (1, 2, 3)]

    def fourth(self):
        total, self.norm = small(
            self.order,
            reduce_fourth_kernel,
            "reduce_fourth",
            [((2, self.rows, D), BF), ((16, D), F32)],
            self.lines,
        )
        total = self.order.tie(total)
        self.ends = [total, to_dp(total), to_core(total)]

    def last(self):
        near = self.order.tie(self.ends[2])
        came = self.order.tie(self.ends[1])
        self.ends = [self.ends[0], came, near, to_core(came)]


def quarter_of(place, ends, quarter, rows):
    core = place[3]
    half, which = quarter >> 1, quarter & 1
    first = jnp.where(place[3] == which, ends[0][core, rows], ends[2][core, rows].astype(BF))
    second = jnp.where(place[3] == which, ends[1][core, rows], ends[3][core, rows])
    return jnp.where(place[2] == half, first, second).astype(F32)


def unpack_kernel(layout, place, *refs):
    ends, outs = refs[:4], refs[4:]
    first = 0
    for kind, row in layout:
        for quarter in range(4):
            if kind == "ffn":
                for j in range(2):
                    block = 2 * quarter + j
                    rows = slice(row + j * BLOCK, row + (j + 1) * BLOCK)
                    value = quarter_of(place, ends, quarter, rows)
                    if block < 4:
                        outs[first][:, block * D : (block + 1) * D] = value
                    else:
                        outs[first + 1][(block - 4) * BLOCK : (block - 3) * BLOCK] = value
            else:
                value = quarter_of(place, ends, quarter, slice(row, row + BLOCK))
                if kind == "attn":
                    if quarter < 3:
                        outs[first][:, quarter * D : (quarter + 1) * D] = value
                    else:
                        outs[first + 1][...] = value
                elif quarter in (1, 2):
                    outs[first + 1][:, (quarter - 1) * D : quarter * D] = value
                else:
                    outs[first + (quarter + 1) // 2][...] = value
        first += 3 if kind == "cross" else 2


SHARD_SHAPES = {
    "ffn": [((BLOCK, FF), F32), ((4 * BLOCK, D), F32)],
    "attn": [((BLOCK, 3 * D), F32), ((BLOCK, D), F32)],
    "cross": [((BLOCK, D), F32), ((BLOCK, 2 * D), F32), ((BLOCK, D), F32)],
}


def unpack(order, place, ends, layout):
    return small(
        order,
        functools.partial(unpack_kernel, layout),
        "unpack",
        [item for kind, unused in layout for item in SHARD_SHAPES[kind]],
        (place, *ends),
        in_specs=[SM] + [VM] * 4,
    )


def norm_last_kernel(place, total, *outs):
    total = total[...]
    spot = place[0] * 4 + place[1] * 2 + place[3]
    turned = jnp.zeros((16, BLOCK), F32)
    for k in range(SHARDS):
        turned = jnp.where(spot == k, total[:, k * BLOCK : (k + 1) * BLOCK], turned)
    for first, gain, bias in ((0, outs[0], outs[1]), (4, outs[2], outs[3])):
        for k in range(gain.shape[0]):
            gain[k : k + 1] = turned[first + 2 * k : first + 2 * k + 1]
            bias[k : k + 1] = turned[first + 2 * k + 1 : first + 2 * k + 2]


def norm_last(order, place, total):
    return small(
        order,
        norm_last_kernel,
        "norm_last",
        [((2, BLOCK), F32), ((2, BLOCK), F32), ((3, BLOCK), F32), ((3, BLOCK), F32)],
        (place, total),
        in_specs=[SM, VM],
    )


def spread_kernel(own, came, ffn_in, ffn_out, cross_q, cross_kv, cross_out):
    total = own[...].astype(F32) + came[...].astype(F32)
    for block in range(4):
        ffn_in[:, block * D : (block + 1) * D] = total[block * BLOCK : (block + 1) * BLOCK]
    ffn_out[...] = total[128:256]
    cross_q[...] = total[256:288]
    cross_kv[:, 0:D] = total[288:320]
    cross_kv[:, D : 2 * D] = total[320:352]
    cross_out[...] = total[352:384]


def spread(order, own, came):
    return small(
        order,
        spread_kernel,
        "spread",
        SHARD_SHAPES["ffn"] + SHARD_SHAPES["cross"],
        (own, came),
    )


def gather_plain(weights):
    parts = []
    for weight in weights:
        whole = lax.all_gather(weight, AXIS, axis=0, tiled=True)
        parts.append(jax.vmap(blocks_of)(whole.reshape(SHARDS, -1, whole.shape[1])))
    return jnp.concatenate(parts, axis=1).reshape(4, 4, -1, D)


def reduce_plain(made, columns):
    shards = made.reshape(SHARDS, -1, BLOCK, D)
    grads = []
    for first, last, cols in columns:
        whole = jax.vmap(functools.partial(shard_of, cols=cols))(shards[:, first:last])
        whole = whole.reshape(-1, cols).astype(F32)
        part = lax.psum_scatter(whole, AXIS, scatter_dimension=0, tiled=True)
        grads.append(lax.psum(part.astype(BF), "dp").astype(F32))
    return grads


def norm_rows_of(gain_enc, bias_enc, gain_dec, bias_dec):
    rows = []
    for gain, bias in ((gain_enc, bias_enc), (gain_dec, bias_dec)):
        for k in range(gain.shape[0]):
            rows += [gain[k : k + 1], bias[k : k + 1]]
    return jnp.concatenate(rows, axis=0)


ATTN_COLUMNS = ((0, 3, 3 * D), (3, 4, D))
FFN_COLUMNS = ((0, 4, FF), (4, 8, D))
CROSS_COLUMNS = ((0, 1, D), (1, 3, 2 * D), (3, 4, D))


def step(
    custom,
    source,
    first_in,
    second_in,
    cot_first,
    cot_second,
    src_lengths,
    tgt_lengths,
    enc_attn_in,
    enc_attn_out,
    enc_ffn_in,
    enc_ffn_out,
    enc_gain,
    enc_bias,
    dec_self_in,
    dec_self_out,
    dec_cross_q,
    dec_cross_kv,
    dec_cross_out,
    dec_ffn_in,
    dec_ffn_out,
    dec_gain,
    dec_bias,
):
    order = Order()
    group_self = (dec_self_in, dec_self_out)
    group_enc = (enc_attn_in, enc_attn_out)
    group_enc_ffn = (enc_ffn_in, enc_ffn_out)
    group_cross = (dec_cross_q, dec_cross_kv, dec_cross_out)
    group_ffn = (dec_ffn_in, dec_ffn_out)
    if custom:
        weights = group_self + group_enc + group_enc_ffn + group_cross + group_ffn
        mine_one, mine_two, mine_three, place = pack(
            order, weights, (enc_gain, enc_bias, dec_gain, dec_bias)
        )
        mine = (mine_one, mine_three)
        pairs = pair_up(order, place, mine, [to_core(x) for x in mine])
        one, three = (Gather(order, pair) for pair in pairs)
        one.along_z()
        one.parts[3] = order.tie(one.parts[3])
        mine_two = order.tie(mine_two)
        whole = lax.all_gather(mine_two, AXIS, axis=0, tiled=True).reshape(4, 4, -1, D)
        one.lined(place)
        one.first_cross()
        three.along_z()
        one.crossed(three.parts)
        one.second_cross()
        three.lined(place)
        three.first_cross()
        one.share()
        one.done()
        gains = first_in
        w_self, w_enc = (Layout(0, 8), one.pieces), (Layout(32, 8), one.pieces)
        w_enc_ffn = (Layout(0, 1), (whole,))
        w_cross = (Layout(256, 1, 1, 256, 384), (whole,))
    else:
        place = jnp.zeros((4,), jnp.int32)
        w_self, w_enc, w_enc_ffn = (
            (Layout(0, 1, 1, 0, rows), (gather_plain(group),))
            for group, rows in ((group_self, 128), (group_enc, 128), (group_enc_ffn, 256))
        )
        w_cross = (Layout(0, 1, 1, 256, 384), (gather_plain(group_cross),))
        w_ffn = (Layout(0, 1, 1, 0, 384), (gather_plain(group_ffn),))
        norm_rows = norm_rows_of(enc_gain, enc_bias, dec_gain, dec_bias)
        gains = lax.all_gather(norm_rows, AXIS, axis=1, tiled=True)
        gains = jnp.pad(gains.astype(F32), ((0, 6), (0, 0)))

    (hidden_one, *kept_self), (hidden_enc, *kept_enc), gains = self_forward(
        order, place, src_lengths, tgt_lengths, gains, [first_in, second_in, source], w_self, w_enc
    )
    if custom:
        three.crossed()
        three.second_cross()
        three.share()
    kept_enc_ffn, kept_cross = second(
        order, place, src_lengths, tgt_lengths, gains, hidden_enc, hidden_one, w_enc_ffn, w_cross
    )
    if custom:
        three.done()
        w_ffn = (Layout(0, 8, 1, 0, 384), three.pieces)
    norm_ffn, norm_cross, first_out, second_out, grad_memory, grad_one, made = middle(
        order, place, gains, hidden_one, kept_cross, (cot_first, cot_second), w_cross, w_ffn
    )
    if custom:
        scattered = lax.psum_scatter(
            made.reshape(-1, D), AXIS, scatter_dimension=0, tiled=True
        )
    grad_enc, norm_enc_ffn, *made_enc_ffn = ffn_back(
        order, 2, place, gains, hidden_enc, grad_memory, kept_enc_ffn, w_enc_ffn
    )
    if custom:
        red = Reduce(order)
        red.add(*made_enc_ffn)
    grad_first, norm_self, *made_self = self_back(
        order, 4, place, gains, [first_in, second_in], grad_one, kept_self, w_self
    )
    if custom:
        red.arrive()
        red.add(*made_self)
    grad_source, norm_total, *made_enc = self_back(
        order,
        0,
        place,
        gains,
        [source],
        grad_enc,
        kept_enc,
        w_enc,
        (norm_enc_ffn, norm_self, norm_cross, norm_ffn),
    )
    if custom:
        red.arrive()
        red.add(*made_enc)
        red.start_norm(norm_total)
        red.first()
        red.second()
        red.third(place)
        scattered = order.tie(scattered)
        scattered_came = order.tie(to_dp(scattered))
        red.fourth()
        grads_ffn_cross = spread(order, scattered, scattered_came)
        norm_grads = norm_last(order, place, red.norm)
        red.last()
        grads_ffn, grads_cross = grads_ffn_cross[:2], grads_ffn_cross[2:]
        g = unpack(order, place, red.ends, (("ffn", 0), ("attn", 64), ("attn", 96)))
        grads_enc_ffn, grads_self, grads_enc = g[:2], g[2:4], g[4:6]
    else:
        grads_ffn = reduce_plain(made[:, :, 0:256], FFN_COLUMNS)
        grads_cross = reduce_plain(made[:, :, 256:384], CROSS_COLUMNS)
        grads_enc_ffn = reduce_plain(*made_enc_ffn, FFN_COLUMNS)
        grads_self = reduce_plain(*made_self, ATTN_COLUMNS)
        grads_enc = reduce_plain(*made_enc, ATTN_COLUMNS)
        norm_shard = lax.psum_scatter(norm_total, AXIS, scatter_dimension=1, tiled=True)
        norm_shard = lax.psum(norm_shard.astype(BF), "dp").astype(F32)
        norm_grads = (norm_shard[0:4:2], norm_shard[1:4:2], norm_shard[4:10:2], norm_shard[5:10:2])
    return (
        first_out,
        second_out,
        grad_source,
        grad_first,
        *grads_enc,
        *grads_enc_ffn,
        *norm_grads[:2],
        *grads_self,
        *grads_cross,
        *grads_ffn,
        *norm_grads[2:],
    )


def solution(mesh):
    blocked = P(("dp", "fsdp"), None)
    rows = P("fsdp", None)
    columns = P(None, "fsdp")
    custom = mesh.shape["fsdp"] == SHARDS and mesh.shape["dp"] == 2
    return jax.shard_map(
        functools.partial(step, custom),
        mesh=mesh,
        in_specs=(blocked,) * 7 + (rows,) * 4 + (columns,) * 2 + (rows,) * 7 + (columns,) * 2,
        out_specs=(blocked,) * 4 + (rows,) * 4 + (columns,) * 2 + (rows,) * 7 + (columns,) * 2,
        check_vma=False,
    )
```

profile of v0, /device:TPU:0, one launch (start us, length us, event | category | flops | bytes accessed | tf_op | source)
XLA Modules:
  0.0 279.2 jit_solution(14334092867910903836)
XLA Ops:
  7.2 2.2 pack.1
  9.4 0.5 collective-permute-start
  10.0 0.1 collective-permute-start.1
  10.0 1.6 collective-permute-done.1.refs_4_
  11.7 1.9 pair_up.1
  13.5 4.8 %collective-permute-start.4 = (bf16[2,80,512]{2,1,0:T(8,128)(2,1)}, bf16[2,80,512]{2,1,0:T(8,128)(2,1)}, u32[]{:S(2)}, u32[]{:S(2)}) collective-permute-start(bf16[2,80,512]{2,1,0:T(8,128)(2,1)} %get-tuple-element.181.refs_1_), channel_id=1, source_target_pairs={{0,12},{1,13},{2,14},{3,15},{4,0},{5,1},{6,2},{7,3},{8,4},{9,5},{1... | collective-permute-start | bytes 491528 | tf_op jit(solution)/shard_map/ppermute | solution.py:790
  18.4 4.2 %collective-permute-done.4.refs_0_ = bf16[2,80,512]{2,1,0:T(8,128)(2,1)} collective-permute-done((bf16[2,80,512]{2,1,0:T(8,128)(2,1)}, bf16[2,80,512]{2,1,0:T(8,128)(2,1)}, u32[]{:S(2)}, u32[]{:S(2)}) %collective-permute-start.4) | collective-permute-done | bytes 163872 | tf_op jit(solution)/shard_map/ppermute | solution.py:790
  22.6 0.0 reduce-scatter.2.cloned.1.call-start
  22.7 1.5 collective-permute-start.3
  24.2 3.4 %collective-permute-start.2 = (bf16[2,80,512]{2,1,0:T(8,128)(2,1)}, bf16[2,80,512]{2,1,0:T(8,128)(2,1)}, u32[]{:S(2)}, u32[]{:S(2)}) collective-permute-start(bf16[2,80,512]{2,1,0:T(8,128)(2,1)} %get-tuple-element.181.refs_1_), channel_id=1, source_target_pairs={{0,4},{1,5},{2,6},{3,7},{4,8},{5,9},{6,10},{7,11},{8,12},{9,13},{1... | collective-permute-start | bytes 491528 | tf_op jit(solution)/shard_map/ppermute | solution.py:790
  27.6 9.0 %collective-permute-done.3.refs_3_ = bf16[2,80,512]{2,1,0:T(8,128)(2,1)} collective-permute-done((bf16[2,80,512]{2,1,0:T(8,128)(2,1)}, bf16[2,80,512]{2,1,0:T(8,128)(2,1)}, u32[]{:S(2)}, u32[]{:S(2)}) %collective-permute-start.3) | collective-permute-done | bytes 163872 | tf_op jit(solution)/shard_map/ppermute | solution.py:790
  36.6 2.6 stack.2
  39.2 1.6 collective-permute-start.6
  40.8 1.5 collective-permute-start.5
  42.3 4.3 %collective-permute-start.8 = (bf16[2,64,512]{2,1,0:T(8,128)(2,1)}, bf16[2,64,512]{2,1,0:T(8,128)(2,1)}, u32[]{:S(2)}, u32[]{:S(2)}) collective-permute-start(bf16[2,64,512]{2,1,0:T(8,128)(2,1)} %get-tuple-element.192.refs_1_), channel_id=1, source_target_pairs={{0,8},{1,9},{2,10},{3,11},{4,12},{5,13},{6,14},{7,15},{8,0},{9,1},... | collective-permute-start | bytes 393224 | tf_op jit(solution)/shard_map/ppermute | solution.py:790
  46.6 2.0 collective-permute-start.7
  48.6 3.4 %collective-permute-done.9.refs_4_ = bf16[2,64,512]{2,1,0:T(8,128)(2,1)} collective-permute-done((bf16[2,64,512]{2,1,0:T(8,128)(2,1)}, bf16[2,64,512]{2,1,0:T(8,128)(2,1)}, u32[]{:S(2)}, u32[]{:S(2)}) %collective-permute-start.9) | collective-permute-done | bytes 131104 | tf_op jit(solution)/shard_map/ppermute | solution.py:790
  52.0 9.1 %collective-permute-done.8.refs_3_ = bf16[2,64,512]{2,1,0:T(8,128)(2,1)} collective-permute-done((bf16[2,64,512]{2,1,0:T(8,128)(2,1)}, bf16[2,64,512]{2,1,0:T(8,128)(2,1)}, u32[]{:S(2)}, u32[]{:S(2)}) %collective-permute-start.8) | collective-permute-done | bytes 131104 | tf_op jit(solution)/shard_map/ppermute | solution.py:790
  61.1 0.1 collective-permute-start.12
  61.2 0.5 collective-permute-start.13
  61.7 1.5 collective-permute-start.10
  63.2 2.5 stack.3
  65.7 13.0 %collective-permute-done.10.refs_0_ = bf16[4,2,80,512]{3,2,1,0:T(8,128)(2,1)} collective-permute-done((bf16[4,2,80,512]{3,2,1,0:T(8,128)(2,1)}, bf16[4,2,80,512]{3,2,1,0:T(8,128)(2,1)}, u32[]{:S(2)}, u32[]{:S(2)}) %collective-permute-start.10) | collective-permute-done | bytes 655392 | tf_op jit(solution)/shard_map/ppermute | solution.py:802
  78.7 0.5 collective-permute-start.18
  79.3 1.3 collective-permute-start.16
  80.6 1.5 collective-permute-start.15
  82.0 10.5 %self_forward.1 = (f32[512,512]{1,0:T(8,128)}, bf16[512,512]{1,0:T(8,128)(2,1)}, bf16[512,1536]{1,0:T(8,128)(2,1)}, bf16[16,256,256]{2,1,0:T(8,128)(2,1)}, bf16[...) custom-call(s32[4]{0:T(128)} %get-tuple-element.175.refs_0_.refs_2_,, ...), custom_call_target="tpu_custom_call", output_to_operand_aliasing={{11}: (23, {})} | custom-call | flops 13210999808 | tf_op jit(solution)/shard_map/self_forward/pallas_call | solution.py:597
  92.5 0.9 collective-permute-done.16.refs_1_
  93.4 1.0 collective-permute-done.15.refs_0_
  94.4 1.5 collective-permute-start.17
  95.9 0.2 collective-permute-start.19
  96.1 0.8 all-gather.2.cloned.1.call-done
  96.9 11.1 %second.1 = (bf16[256,512]{1,0:T(8,128)(2,1)}, bf16[256,2048]{1,0:T(8,128)(2,1)}, bf16[256,2048]{1,0:T(8,128)(2,1)}, bf16[256,512]{1,0:T(8,128)(2,1)}, bf16[512,...) custom-call(s32[4]{0:T(128)} %get-tuple-element.175.refs_0_.refs_2_,, ...), custom_call_target="tpu_custom_call", output_to_operand_aliasing={{10}: (8, {})} | custom-call | flops 14311000064 | tf_op jit(solution)/shard_map/second/pallas_call | solution.py:597
  108.1 1.0 collective-permute-done.17.refs_0_
  109.1 2.2 collective-permute-done.21.refs_0_
  111.3 21.3 %middle.1 = (f32[2,512]{1,0:T(2,128)}, f32[2,512]{1,0:T(2,128)}, bf16[256,512]{1,0:T(8,128)(2,1)}, bf16[256,512]{1,0:T(8,128)(2,1)}, f32[256,512]{1,0:T(8,128)},...) custom-call(s32[4]{0:T(128)} %get-tuple-element.175.refs_0_.refs_2_,, ...), custom_call_target="tpu_custom_call", output_to_operand_aliasing={{7}: (21, {})} | custom-call | flops 27510999040 | tf_op jit(solution)/shard_map/middle/pallas_call | solution.py:597
  132.7 10.2 %ffn_back.1 = (f32[256,512]{1,0:T(8,128)}, f32[2,512]{1,0:T(2,128)}, bf16[2,2,4,2,64,512]{5,4,3,2,1,0:T(8,128)(2,1)}, bf16[2,2,4,2,64,512]{5,4,3,2,1,0:T(8,128)(2,1)}, f32[8,128]{1,0:T(8,128)}) custom-call(s32[4]{0:T(128)} %get-tuple-element.175.refs_0_.refs_2_, f32[16,512]{1,0:T(8,128)} %get-tuple-element.210.refs_3_.refs_1_, ...), custom_call_target="tpu_custom_call", output_to_operand_aliasing={{4}: (8, {})} | custom-call | flops 11230999552 | tf_op jit(solution)/shard_map/ffn_back/pallas_call | solution.py:597
  142.9 0.2 collective-permute-start.22
  143.1 13.3 %self_back.2 = (f32[256,512]{1,0:T(8,128)}, f32[2,512]{1,0:T(2,128)}, bf16[2,2,4,2,32,512]{5,4,3,2,1,0:T(8,128)(2,1)}, bf16[2,2,4,2,32,512]{5,4,3,2,1,0:T(8,128)(2,1)}, f32[8,128]{1,0:T(8,128)}) custom-call(s32[4]{0:T(128)} %get-tuple-element.175.refs_0_.refs_2_, f32[16,512]{1,0:T(8,128)} %get-tuple-element.210.refs_3_.refs_1_, ...), custom_call_target="tpu_custom_call", output_to_operand_aliasing={{4}: (17, {})} | custom-call | flops 13870999552 | tf_op jit(solution)/shard_map/self_back/pallas_call | solution.py:597
  156.5 0.4 collective-permute-start.23
  156.9 9.0 %self_back.3 = (f32[256,512]{1,0:T(8,128)}, f32[16,512]{1,0:T(8,128)}, bf16[2,2,4,2,32,512]{5,4,3,2,1,0:T(8,128)(2,1)}, bf16[2,2,4,2,32,512]{5,4,3,2,1,0:T(8,128)(2,1)}, f32[8,128]{1,0:T(8,128)}) custom-call(s32[4]{0:T(128)} %get-tuple-element.175.refs_0_.refs_2_, f32[16,512]{1,0:T(8,128)} %get-tuple-element.210.refs_3_.refs_1_, ...), custom_call_target="tpu_custom_call", output_to_operand_aliasing={{4}: (20, {})} | custom-call | flops 10131000320 | tf_op jit(solution)/shard_map/self_back/pallas_call | solution.py:597
  166.0 0.2 collective-permute-start.25
  166.2 0.4 collective-permute-start.24
  166.5 2.5 collective-permute-done.24.refs_1_
  169.1 4.1 %reduce_first.1 = (bf16[2064,512]{1,0:T(8,128)(2,1)}, f32[8,128]{1,0:T(8,128)}) custom-call(f32[16,512]{1,0:T(8,128)} %get-tuple-element.271.refs_0_, f32[16,512]{1,0:T(8,128)} %collective-permute-done.24.refs_1_, bf16[2,2,4,2,64,512]{5,4,3,2,1,0:T(8,128)(2,1)} %get-tuple-element.272.refs_2_.refs_3_.refs_5_, ...), custom_call_target="tpu_custom_call", output_to_operand_aliasing={{1}: (8, {})} | custom-call | flops 11000000 | tf_op jit(solution)/shard_map/reduce_first/pallas_call | solution.py:597
  173.2 0.8 collective-permute-start.26
  174.0 36.7 %collective-permute-done.26.refs_1_.refs_2_.refs_3_ = bf16[2064,512]{1,0:T(8,128)(2,1)} collective-permute-done((bf16[2064,512]{1,0:T(8,128)(2,1)}, bf16[2064,512]{1,0:T(8,128)(2,1)}, u32[]{:S(2)}, u32[]{:S(2)}) %collective-permute-start.26) | collective-permute-done | bytes 2113568 | tf_op jit(solution)/shard_map/ppermute | solution.py:806
  210.7 3.6 %reduce_second.1 = (bf16[1040,512]{1,0:T(8,128)(2,1)}, f32[8,128]{1,0:T(8,128)}) custom-call(bf16[2064,512]{1,0:T(8,128)(2,1)} %get-tuple-element.281.refs_0_, bf16[2064,512]{1,0:T(8,128)(2,1)} %collective-permute-done.26.refs_1_.refs_2_.refs_3_, bf16[2064,512]{1,0:T(8,128)(2,1)} %collective-permute-done.26.refs_1_.refs_2_.refs_3_, ...), custom_call_target="tpu_custom_call", output_to_operand_aliasing={{1}: (9, {})} | custom-call | flops 11000000 | tf_op jit(solution)/shard_map/reduce_second/pallas_call | solution.py:597
  214.3 1.6 collective-permute-start.27
  215.9 13.8 %collective-permute-done.27.refs_1_.refs_4_ = bf16[1040,512]{1,0:T(8,128)(2,1)} collective-permute-done((bf16[1040,512]{1,0:T(8,128)(2,1)}, bf16[1040,512]{1,0:T(8,128)(2,1)}, u32[]{:S(2)}, u32[]{:S(2)}) %collective-permute-start.27) | collective-permute-done | bytes 1064992 | tf_op jit(solution)/shard_map/ppermute | solution.py:812
  229.7 3.9 %reduce_third.1 = (bf16[272,512]{1,0:T(8,128)(2,1)}, bf16[272,512]{1,0:T(8,128)(2,1)}, bf16[272,512]{1,0:T(8,128)(2,1)}, bf16[272,512]{1,0:T(8,128)(2,1)}, f32[8,128]{1,0:T(8,128)}) custom-call(bf16[1040,512]{1,0:T(8,128)(2,1)} %get-tuple-element.285.refs_0_, ...), custom_call_target="tpu_custom_call", output_to_operand_aliasing={{4}: (11, {})} | custom-call | flops 11000000 | tf_op jit(solution)/shard_map/reduce_third/pallas_call | solution.py:597
  233.6 1.6 collective-permute-start.31
  235.2 4.6 %collective-permute-start.30 = (bf16[272,512]{1,0:T(8,128)(2,1)}, bf16[272,512]{1,0:T(8,128)(2,1)}, u32[]{:S(2)}, u32[]{:S(2)}) collective-permute-start(bf16[272,512]{1,0:T(8,128)(2,1)} %get-tuple-element.298), channel_id=1, source_target_pairs={{0,12},{1,13},{2,14},{3,15},{4,0},{5,1},{6,2},{7,3},{8,4},{9,5},{1... | collective-permute-start | bytes 835592 | tf_op jit(solution)/shard_map/ppermute | solution.py:790
  239.7 0.6 collective-permute-start.28
  240.3 1.5 collective-permute-done.31.refs_0_
  241.8 4.8 %collective-permute-done.30.refs_3_ = bf16[272,512]{1,0:T(8,128)(2,1)} collective-permute-done((bf16[272,512]{1,0:T(8,128)(2,1)}, bf16[272,512]{1,0:T(8,128)(2,1)}, u32[]{:S(2)}, u32[]{:S(2)}) %collective-permute-start.30) | collective-permute-done | bytes 278560 | tf_op jit(solution)/shard_map/ppermute | solution.py:790
  246.5 10.4 %collective-permute-done.29.refs_2_ = bf16[272,512]{1,0:T(8,128)(2,1)} collective-permute-done((bf16[272,512]{1,0:T(8,128)(2,1)}, bf16[272,512]{1,0:T(8,128)(2,1)}, u32[]{:S(2)}, u32[]{:S(2)}) %collective-permute-start.29) | collective-permute-done | bytes 278560 | tf_op jit(solution)/shard_map/ppermute | solution.py:790
  257.0 2.0 reduce_fourth.1
  259.0 0.6 collective-permute-start.32
  259.6 2.0 spread.1
  261.6 2.5 norm_last.1
  264.0 4.0 %collective-permute-done.32.refs_0_ = bf16[2,128,512]{2,1,0:T(8,128)(2,1)} collective-permute-done((bf16[2,128,512]{2,1,0:T(8,128)(2,1)}, bf16[2,128,512]{2,1,0:T(8,128)(2,1)}, u32[]{:S(2)}, u32[]{:S(2)}) %collective-permute-start.32) | collective-permute-done | bytes 262176 | tf_op jit(solution)/shard_map/ppermute | solution.py:802
  268.0 1.9 collective-permute-done.34.refs_4_
  269.9 2.3 unpack.1
  (58 shorter events, 0.2 us)
Async XLA Ops:
  7.2 89.7 %all-gather.2.cloned.1.call-start = ((), (), s32[]{:S(2)}) async-start(), calls=%async_computation.1 | async-start | bytes 6684672 | tf_op jit(solution)/shard_map/all_gather | solution.py:1351
  9.4 2.2 collective-permute-start
  10.0 1.7 collective-permute-start.1
  13.5 9.0 %collective-permute-start.4 = (bf16[2,80,512]{2,1,0:T(8,128)(2,1)}, bf16[2,80,512]{2,1,0:T(8,128)(2,1)}, u32[]{:S(2)}, u32[]{:S(2)}) collective-permute-start(bf16[2,80,512]{2,1,0:T(8,128)(2,1)} %get-tuple-element.181.refs_1_), channel_id=1, source_target_pairs={{0,12},{1,13},{2,14},{3,15},{4,0},{5,1},{6,2},{7,3},{8,4},{9,5},{1... | collective-permute-start | bytes 491528 | tf_op jit(solution)/shard_map/ppermute | solution.py:790
  22.6 211.0 %reduce-scatter.2.cloned.1.call-start = ((), (), s32[]{:S(2)}) async-start(), calls=%async_computation.2 | async-start | bytes 6684672 | tf_op jit(solution)/shard_map/reduce_scatter | solution.py:1394
  22.7 14.0 %collective-permute-start.3 = (bf16[2,80,512]{2,1,0:T(8,128)(2,1)}, bf16[2,80,512]{2,1,0:T(8,128)(2,1)}, u32[]{:S(2)}, u32[]{:S(2)}) collective-permute-start(bf16[2,80,512]{2,1,0:T(8,128)(2,1)} %get-tuple-element.181.refs_1_), channel_id=1, source_target_pairs={{0,8},{1,9},{2,10},{3,11},{4,12},{5,13},{6,14},{7,15},{8,0},{9,1},... | collective-permute-start | bytes 491528 | tf_op jit(solution)/shard_map/ppermute | solution.py:790
  24.2 12.4 %collective-permute-start.2 = (bf16[2,80,512]{2,1,0:T(8,128)(2,1)}, bf16[2,80,512]{2,1,0:T(8,128)(2,1)}, u32[]{:S(2)}, u32[]{:S(2)}) collective-permute-start(bf16[2,80,512]{2,1,0:T(8,128)(2,1)} %get-tuple-element.181.refs_1_), channel_id=1, source_target_pairs={{0,4},{1,5},{2,6},{3,7},{4,8},{5,9},{6,10},{7,11},{8,12},{9,13},{1... | collective-permute-start | bytes 491528 | tf_op jit(solution)/shard_map/ppermute | solution.py:790
  39.2 21.9 %collective-permute-start.6 = (bf16[4,2,80,512]{3,2,1,0:T(8,128)(2,1)}, bf16[4,2,80,512]{3,2,1,0:T(8,128)(2,1)}, u32[]{:S(2)}, u32[]{:S(2)}) collective-permute-start(bf16[4,2,80,512]{3,2,1,0:T(8,128)(2,1)} %get-tuple-element.189.refs_7_.refs_15_.refs_9_.refs_12_), channel_id=1, source_target_pairs={{0,2},{1,3},{2,0},{3,1},{4,6},{5,7},{6,4},{7,5},{8,10},{9,11},{10,... | collective-permute-start | bytes 1966088 | tf_op jit(solution)/shard_map/ppermute | solution.py:798
  40.8 20.3 %collective-permute-start.5 = (bf16[4,2,80,512]{3,2,1,0:T(8,128)(2,1)}, bf16[4,2,80,512]{3,2,1,0:T(8,128)(2,1)}, u32[]{:S(2)}, u32[]{:S(2)}) collective-permute-start(bf16[4,2,80,512]{3,2,1,0:T(8,128)(2,1)} %get-tuple-element.189.refs_7_.refs_15_.refs_9_.refs_12_), channel_id=1, source_target_pairs={{0,16},{1,17},{2,18},{3,19},{4,20},{5,21},{6,22},{7,23},{8,24},{9,... | collective-permute-start | bytes 1966088 | tf_op jit(solution)/shard_map/ppermute | solution.py:802
  42.3 9.7 %collective-permute-start.9 = (bf16[2,64,512]{2,1,0:T(8,128)(2,1)}, bf16[2,64,512]{2,1,0:T(8,128)(2,1)}, u32[]{:S(2)}, u32[]{:S(2)}) collective-permute-start(bf16[2,64,512]{2,1,0:T(8,128)(2,1)} %get-tuple-element.192.refs_1_), channel_id=1, source_target_pairs={{0,12},{1,13},{2,14},{3,15},{4,0},{5,1},{6,2},{7,3},{8,4},{9,5},{1... | collective-permute-start | bytes 393224 | tf_op jit(solution)/shard_map/ppermute | solution.py:790
  42.3 18.8 %collective-permute-start.8 = (bf16[2,64,512]{2,1,0:T(8,128)(2,1)}, bf16[2,64,512]{2,1,0:T(8,128)(2,1)}, u32[]{:S(2)}, u32[]{:S(2)}) collective-permute-start(bf16[2,64,512]{2,1,0:T(8,128)(2,1)} %get-tuple-element.192.refs_1_), channel_id=1, source_target_pairs={{0,8},{1,9},{2,10},{3,11},{4,12},{5,13},{6,14},{7,15},{8,0},{9,1},... | collective-permute-start | bytes 393224 | tf_op jit(solution)/shard_map/ppermute | solution.py:790
  46.6 14.5 %collective-permute-start.7 = (bf16[2,64,512]{2,1,0:T(8,128)(2,1)}, bf16[2,64,512]{2,1,0:T(8,128)(2,1)}, u32[]{:S(2)}, u32[]{:S(2)}) collective-permute-start(bf16[2,64,512]{2,1,0:T(8,128)(2,1)} %get-tuple-element.192.refs_1_), channel_id=1, source_target_pairs={{0,4},{1,5},{2,6},{3,7},{4,8},{5,9},{6,10},{7,11},{8,12},{9,13},{1... | collective-permute-start | bytes 393224 | tf_op jit(solution)/shard_map/ppermute | solution.py:790
  52.0 13.7 %collective-permute-start.11 = (bf16[4,2,80,512]{3,2,1,0:T(8,128)(2,1)}, bf16[4,2,80,512]{3,2,1,0:T(8,128)(2,1)}, u32[]{:S(2)}, u32[]{:S(2)}) collective-permute-start(bf16[4,2,80,512]{3,2,1,0:T(8,128)(2,1)} %get-tuple-element.189.refs_7_.refs_15_.refs_9_.refs_12_), channel_id=1, source_target_pairs={{0,1},{1,0},{2,3},{3,2},{4,5},{5,4},{6,7},{7,6},{8,9},{9,8},{10,11... | collective-permute-start | bytes 1966088 | tf_op jit(solution)/shard_map/ppermute | solution.py:786
  61.1 4.5 %collective-permute-start.12 = (bf16[4,2,80,512]{3,2,1,0:T(8,128)(2,1)}, bf16[4,2,80,512]{3,2,1,0:T(8,128)(2,1)}, u32[]{:S(2)}, u32[]{:S(2)}) collective-permute-start(bf16[4,2,80,512]{3,2,1,0:T(8,128)(2,1)} %get-tuple-element.194.refs_8_.refs_16_.refs_10_.refs_13_), channel_id=1, source_target_pairs={{0,1},{1,0},{2,3},{3,2},{4,5},{5,4},{6,7},{7,6},{8,9},{9,8},{10,11... | collective-permute-start | bytes 1966088 | tf_op jit(solution)/shard_map/ppermute | solution.py:786
  61.2 4.5 %collective-permute-start.13 = (bf16[4,2,80,512]{3,2,1,0:T(8,128)(2,1)}, bf16[4,2,80,512]{3,2,1,0:T(8,128)(2,1)}, u32[]{:S(2)}, u32[]{:S(2)}) collective-permute-start(bf16[4,2,80,512]{3,2,1,0:T(8,128)(2,1)} %get-tuple-element.195.refs_9_.refs_17_.refs_11_.refs_14_), channel_id=1, source_target_pairs={{0,1},{1,0},{2,3},{3,2},{4,5},{5,4},{6,7},{7,6},{8,9},{9,8},{10,11... | collective-permute-start | bytes 1966088 | tf_op jit(solution)/shard_map/ppermute | solution.py:786
  61.7 17.0 %collective-permute-start.10 = (bf16[4,2,80,512]{3,2,1,0:T(8,128)(2,1)}, bf16[4,2,80,512]{3,2,1,0:T(8,128)(2,1)}, u32[]{:S(2)}, u32[]{:S(2)}) collective-permute-start(bf16[4,2,80,512]{3,2,1,0:T(8,128)(2,1)} %get-tuple-element.195.refs_9_.refs_17_.refs_11_.refs_14_), channel_id=1, source_target_pairs={{0,16},{1,17},{2,18},{3,19},{4,20},{5,21},{6,22},{7,23},{8,24},{9,... | collective-permute-start | bytes 1966088 | tf_op jit(solution)/shard_map/ppermute | solution.py:802
  78.7 3.3 %collective-permute-start.14 = (bf16[4,2,80,512]{3,2,1,0:T(8,128)(2,1)}, bf16[4,2,80,512]{3,2,1,0:T(8,128)(2,1)}, u32[]{:S(2)}, u32[]{:S(2)}) collective-permute-start(bf16[4,2,80,512]{3,2,1,0:T(8,128)(2,1)} %get-tuple-element.203.refs_10_.refs_18_.refs_12_.refs_15_), channel_id=1, source_target_pairs={{0,1},{1,0},{2,3},{3,2},{4,5},{5,4},{6,7},{7,6},{8,9},{9,8},{10,11... | collective-permute-start | bytes 1966088 | tf_op jit(solution)/shard_map/ppermute | solution.py:786
  78.7 29.3 %collective-permute-start.18 = (bf16[4,2,64,512]{3,2,1,0:T(8,128)(2,1)}, bf16[4,2,64,512]{3,2,1,0:T(8,128)(2,1)}, u32[]{:S(2)}, u32[]{:S(2)}) collective-permute-start(bf16[4,2,64,512]{3,2,1,0:T(8,128)(2,1)} %get-tuple-element.214.refs_13_), channel_id=1, source_target_pairs={{0,1},{1,0},{2,3},{3,2},{4,5},{5,4},{6,7},{7,6},{8,9},{9,8},{10,11... | collective-permute-start | bytes 1572872 | tf_op jit(solution)/shard_map/ppermute | solution.py:786
  79.3 14.1 %collective-permute-start.16 = (bf16[4,2,64,512]{3,2,1,0:T(8,128)(2,1)}, bf16[4,2,64,512]{3,2,1,0:T(8,128)(2,1)}, u32[]{:S(2)}, u32[]{:S(2)}) collective-permute-start(bf16[4,2,64,512]{3,2,1,0:T(8,128)(2,1)} %get-tuple-element.214.refs_13_), channel_id=1, source_target_pairs={{0,2},{1,3},{2,0},{3,1},{4,6},{5,7},{6,4},{7,5},{8,10},{9,11},{10,... | collective-permute-start | bytes 1572872 | tf_op jit(solution)/shard_map/ppermute | solution.py:798
  80.6 13.9 %collective-permute-start.15 = (bf16[4,2,64,512]{3,2,1,0:T(8,128)(2,1)}, bf16[4,2,64,512]{3,2,1,0:T(8,128)(2,1)}, u32[]{:S(2)}, u32[]{:S(2)}) collective-permute-start(bf16[4,2,64,512]{3,2,1,0:T(8,128)(2,1)} %get-tuple-element.214.refs_13_), channel_id=1, source_target_pairs={{0,16},{1,17},{2,18},{3,19},{4,20},{5,21},{6,22},{7,23},{8,24},{9,... | collective-permute-start | bytes 1572872 | tf_op jit(solution)/shard_map/ppermute | solution.py:802
  94.4 13.6 %collective-permute-start.20 = (bf16[4,2,64,512]{3,2,1,0:T(8,128)(2,1)}, bf16[4,2,64,512]{3,2,1,0:T(8,128)(2,1)}, u32[]{:S(2)}, u32[]{:S(2)}) collective-permute-start(bf16[4,2,64,512]{3,2,1,0:T(8,128)(2,1)} %get-tuple-element.225.refs_15_), channel_id=1, source_target_pairs={{0,1},{1,0},{2,3},{3,2},{4,5},{5,4},{6,7},{7,6},{8,9},{9,8},{10,11... | collective-permute-start | bytes 1572872 | tf_op jit(solution)/shard_map/ppermute | solution.py:786
  94.4 14.7 %collective-permute-start.17 = (bf16[4,2,64,512]{3,2,1,0:T(8,128)(2,1)}, bf16[4,2,64,512]{3,2,1,0:T(8,128)(2,1)}, u32[]{:S(2)}, u32[]{:S(2)}) collective-permute-start(bf16[4,2,64,512]{3,2,1,0:T(8,128)(2,1)} %get-tuple-element.225.refs_15_), channel_id=1, source_target_pairs={{0,16},{1,17},{2,18},{3,19},{4,20},{5,21},{6,22},{7,23},{8,24},{9,... | collective-permute-start | bytes 1572872 | tf_op jit(solution)/shard_map/ppermute | solution.py:802
  95.9 12.1 %collective-permute-start.19 = (bf16[4,2,64,512]{3,2,1,0:T(8,128)(2,1)}, bf16[4,2,64,512]{3,2,1,0:T(8,128)(2,1)}, u32[]{:S(2)}, u32[]{:S(2)}) collective-permute-start(bf16[4,2,64,512]{3,2,1,0:T(8,128)(2,1)} %get-tuple-element.224.refs_14_), channel_id=1, source_target_pairs={{0,1},{1,0},{2,3},{3,2},{4,5},{5,4},{6,7},{7,6},{8,9},{9,8},{10,11... | collective-permute-start | bytes 1572872 | tf_op jit(solution)/shard_map/ppermute | solution.py:786
  109.1 2.3 collective-permute-start.21
  142.9 13.5 %collective-permute-start.22 = (bf16[2,2,4,2,64,512]{5,4,3,2,1,0:T(8,128)(2,1)}, bf16[2,2,4,2,64,512]{5,4,3,2,1,0:T(8,128)(2,1)}, u32[]{:S(2)}, u32[]{:S(2)}) collective-permute-start(bf16[2,2,4,2,64,512]{5,4,3,2,1,0:T(8,128)(2,1)} %get-tuple-element.259), channel_id=1, source_target_pairs={{0,1},{1,0},{2,3},{3,2},{4,5},{5,4},{6,7},{7,6},{8,9},{9,8},{10,11... | collective-permute-start | bytes 6291464 | tf_op jit(solution)/shard_map/ppermute | solution.py:786
  156.5 9.5 %collective-permute-start.23 = (bf16[2,2,4,2,32,512]{5,4,3,2,1,0:T(8,128)(2,1)}, bf16[2,2,4,2,32,512]{5,4,3,2,1,0:T(8,128)(2,1)}, u32[]{:S(2)}, u32[]{:S(2)}) collective-permute-start(bf16[2,2,4,2,32,512]{5,4,3,2,1,0:T(8,128)(2,1)} %get-tuple-element.267), channel_id=1, source_target_pairs={{0,1},{1,0},{2,3},{3,2},{4,5},{5,4},{6,7},{7,6},{8,9},{9,8},{10,11... | collective-permute-start | bytes 3145736 | tf_op jit(solution)/shard_map/ppermute | solution.py:786
  166.0 3.1 %collective-permute-start.25 = (bf16[2,2,4,2,32,512]{5,4,3,2,1,0:T(8,128)(2,1)}, bf16[2,2,4,2,32,512]{5,4,3,2,1,0:T(8,128)(2,1)}, u32[]{:S(2)}, u32[]{:S(2)}) collective-permute-start(bf16[2,2,4,2,32,512]{5,4,3,2,1,0:T(8,128)(2,1)} %get-tuple-element.277), channel_id=1, source_target_pairs={{0,1},{1,0},{2,3},{3,2},{4,5},{5,4},{6,7},{7,6},{8,9},{9,8},{10,11... | collective-permute-start | bytes 3145736 | tf_op jit(solution)/shard_map/ppermute | solution.py:786
  166.2 2.9 %collective-permute-start.24 = (f32[16,512]{1,0:T(8,128)}, f32[16,512]{1,0:T(8,128)}, u32[]{:S(2)}, u32[]{:S(2)}) collective-permute-start(f32[16,512]{1,0:T(8,128)} %get-tuple-element.271.refs_0_), channel_id=1, source_target_pairs={{0,1},{1,0},{2,3},{3,2},{4,5},{5,4},{6,7},{7,6},{8,9},{9,8},{10,11... | collective-permute-start | bytes 98312 | tf_op jit(solution)/shard_map/ppermute | solution.py:786
  173.2 37.5 %collective-permute-start.26 = (bf16[2064,512]{1,0:T(8,128)(2,1)}, bf16[2064,512]{1,0:T(8,128)(2,1)}, u32[]{:S(2)}, u32[]{:S(2)}) collective-permute-start(bf16[2064,512]{1,0:T(8,128)(2,1)} %get-tuple-element.281.refs_0_), channel_id=1, source_target_pairs={{0,2},{1,17},{2,0},{3,19},{4,6},{5,21},{6,4},{7,23},{8,10},{9,25},... | collective-permute-start | bytes 6340616 | tf_op jit(solution)/shard_map/ppermute | solution.py:806
  214.3 15.4 %collective-permute-start.27 = (bf16[1040,512]{1,0:T(8,128)(2,1)}, bf16[1040,512]{1,0:T(8,128)(2,1)}, u32[]{:S(2)}, u32[]{:S(2)}) collective-permute-start(bf16[1040,512]{1,0:T(8,128)(2,1)} %get-tuple-element.285.refs_0_), channel_id=1, source_target_pairs={{0,16},{1,3},{2,18},{3,1},{4,20},{5,7},{6,22},{7,5},{8,24},{9,11},... | collective-permute-start | bytes 3194888 | tf_op jit(solution)/shard_map/ppermute | solution.py:812
  233.6 8.2 %collective-permute-start.31 = (bf16[384,512]{1,0:T(8,128)(2,1)}, bf16[384,512]{1,0:T(8,128)(2,1)}, u32[]{:S(2)}, u32[]{:S(2)}) collective-permute-start(bf16[384,512]{1,0:T(8,128)(2,1)} %get-tuple-element.301.refs_0_), channel_id=1, source_target_pairs={{0,16},{1,17},{2,18},{3,19},{4,20},{5,21},{6,22},{7,23},{8,24},{9,... | collective-permute-start | bytes 1179656 | tf_op jit(solution)/shard_map/ppermute | solution.py:802
  235.2 11.4 %collective-permute-start.30 = (bf16[272,512]{1,0:T(8,128)(2,1)}, bf16[272,512]{1,0:T(8,128)(2,1)}, u32[]{:S(2)}, u32[]{:S(2)}) collective-permute-start(bf16[272,512]{1,0:T(8,128)(2,1)} %get-tuple-element.298), channel_id=1, source_target_pairs={{0,12},{1,13},{2,14},{3,15},{4,0},{5,1},{6,2},{7,3},{8,4},{9,5},{1... | collective-permute-start | bytes 835592 | tf_op jit(solution)/shard_map/ppermute | solution.py:790
  239.7 17.2 %collective-permute-start.29 = (bf16[272,512]{1,0:T(8,128)(2,1)}, bf16[272,512]{1,0:T(8,128)(2,1)}, u32[]{:S(2)}, u32[]{:S(2)}) collective-permute-start(bf16[272,512]{1,0:T(8,128)(2,1)} %get-tuple-element.295), channel_id=1, source_target_pairs={{0,8},{1,9},{2,10},{3,11},{4,12},{5,13},{6,14},{7,15},{8,0},{9,1},... | collective-permute-start | bytes 835592 | tf_op jit(solution)/shard_map/ppermute | solution.py:790
  239.7 17.2 %collective-permute-start.28 = (bf16[272,512]{1,0:T(8,128)(2,1)}, bf16[272,512]{1,0:T(8,128)(2,1)}, u32[]{:S(2)}, u32[]{:S(2)}) collective-permute-start(bf16[272,512]{1,0:T(8,128)(2,1)} %get-tuple-element.292), channel_id=1, source_target_pairs={{0,4},{1,5},{2,6},{3,7},{4,8},{5,9},{6,10},{7,11},{8,12},{9,13},{1... | collective-permute-start | bytes 835592 | tf_op jit(solution)/shard_map/ppermute | solution.py:790
  259.0 5.0 %collective-permute-start.33 = (bf16[2,128,512]{2,1,0:T(8,128)(2,1)}, bf16[2,128,512]{2,1,0:T(8,128)(2,1)}, u32[]{:S(2)}, u32[]{:S(2)}) collective-permute-start(bf16[2,128,512]{2,1,0:T(8,128)(2,1)} %get-tuple-element.306.refs_1_), channel_id=1, source_target_pairs={{0,1},{1,0},{2,3},{3,2},{4,5},{5,4},{6,7},{7,6},{8,9},{9,8},{10,11... | collective-permute-start | bytes 786440 | tf_op jit(solution)/shard_map/ppermute | solution.py:786
  259.0 9.0 %collective-permute-start.32 = (bf16[2,128,512]{2,1,0:T(8,128)(2,1)}, bf16[2,128,512]{2,1,0:T(8,128)(2,1)}, u32[]{:S(2)}, u32[]{:S(2)}) collective-permute-start(bf16[2,128,512]{2,1,0:T(8,128)(2,1)} %get-tuple-element.306.refs_1_), channel_id=1, source_target_pairs={{0,16},{1,17},{2,18},{3,19},{4,20},{5,21},{6,22},{7,23},{8,24},{9,... | collective-permute-start | bytes 786440 | tf_op jit(solution)/shard_map/ppermute | solution.py:802
  268.0 1.9 collective-permute-start.34
Sparse Core Ops, SparseCore 0:
  22.7 74.1 all-gather.1
  132.8 95.0 reduce-scatter.1
where the time goes:
time: 282 us; the launch traced here: 279 us
  waiting for transfers between devices  122 us (43%)
  Pallas kernels  105 us (37%)
  starting transfers between devices  37.7 us (13%)
  between operations  14.6 us (5%)
    pallas_call x17, Pallas kernels, call(): pl.pallas_call(ordered, name=name, out_shape=out_shape + [jax.ShapeDtypeS...  105 us
    ppermute x9, waiting for transfers between devices, to_z(): lax.ppermute(x, BOTH, route(lambda dp, z, y, core: (dp, z + step, y, core)))  40.9 us
    ppermute x1, waiting for transfers between devices, to_yx(): lax.ppermute(x, BOTH, route(lambda dp, z, y, core: (dp, z, y ^ 1, core) i...  36.7 us
    ppermute x9, starting transfers between devices, to_z(): lax.ppermute(x, BOTH, route(lambda dp, z, y, core: (dp, z + step, y, core)))  21.2 us
    ppermute x6, waiting for transfers between devices, to_dp(): lax.ppermute(x, BOTH, route(lambda dp, z, y, core: (1 - dp, z, y, core)))  20.6 us
    ppermute x1, waiting for transfers between devices, to_xy(): lax.ppermute(x, BOTH, route(lambda dp, z, y, core: (dp ^ 1, z, y, core) i...  13.8 us
    ppermute x16, waiting for transfers between devices, to_core(): lax.ppermute(x, BOTH, route(lambda dp, z, y, core: (dp, z, y, 1 - core)))  8.3 us
    ppermute x6, starting transfers between devices, to_dp(): lax.ppermute(x, BOTH, route(lambda dp, z, y, core: (1 - dp, z, y, core)))  8.01 us
  transfers between devices with their start and end apart: 37, of which 19 were waited for; matrix products, arithmetic and copies ran while one was open for 0% of the time, Pallas kernels for 27%

commit v1 on v0

--- a/solution.py
+++ b/solution.py
@@ -200,6 +200,19 @@
             for quarter in (q for q in quarters if q < 4):
                 part = pl.ds(layout.made_offset + quarter * rows, rows)
                 self.store(held.at[:, :, pl.ds(quarter * rows, rows)], outs[0].at[:, :, part])
+        elif 4 in quarters and layout.made == 4:
+            for part in range(2):
+                for turn in range(2):
+                    for first in range(2):
+                        for second in range(2):
+                            y, half, which = place_of(place, turn, first, second)
+                            if part == 0:
+                                y, half = place[1] ^ second, place[2] ^ first
+                            row = pl.multiple_of((2 * half + which) * rows + part * (rows // 2), 16)
+                            self.store(
+                                held.at[:, pl.ds(2 * y, 2), pl.ds(row, rows // 2)],
+                                outs[2 * part + turn].at[first, second],
+                            )
         elif 4 in quarters:
             for turn in range(2):
                 for first in range(2):
@@ -554,7 +567,8 @@
 def made_of(layout, blocks):
     if layout.made == 1:
         return [jax.ShapeDtypeStruct((4, 4, layout.made_rows, D), BF)]
-    return [jax.ShapeDtypeStruct((2, 2, 4, 2, blocks * BLOCK // 4, D), BF)] * 2
+    rows = blocks * BLOCK // (2 * layout.made)
+    return [jax.ShapeDtypeStruct((2, 2, 4, 2, rows, D), BF)] * layout.made
 
 
 def shape(rows, cols, dtype):
@@ -990,11 +1004,18 @@
     return total.astype(BF)
 
 
-def rows_of(parts):
-    row = 0
-    for k, part in enumerate(parts[::2]):
-        yield slice(row, row + part.shape[4]), part, parts[2 * k + 1]
-        row += part.shape[4]
+class Span(typing.NamedTuple):
+    group: int
+    start: int
+    size: int
+    of: int
+    place: int
+
+    def within(self, block):
+        return slice(block * self.of + self.start, block * self.of + self.start + self.size)
+
+    def overall(self, block, rows):
+        return slice(block * rows + self.place, block * rows + self.place + self.size)
 
 
 def send_block(step, source, target, sems, more):
@@ -1004,71 +1025,83 @@
                 source.at[k], target.at[pl.ds(k * source.shape[1], source.shape[1])], sems.at[k]
             )
 
-    last = pltpu.make_async_copy(*more, sems.at[4])
+    last = pltpu.make_async_copy(*more, sems.at[4]) if more else None
     for k, copy in copies():
         pl.when(step == k)(copy.start)
-    pl.when(step == 0)(last.start)
+    if last:
+        pl.when(step == 0)(last.start)
 
     @pl.when(step == 3)
     def _():
         for unused, copy in copies():
             copy.wait()
-        last.wait()
-
-
-def reduce_first_kernel(norm_own, norm_came, *refs):
+        if last:
+            last.wait()
+
+
+def reduce_first_kernel(spans, norms, *refs):
+    norm_parts, parts = refs[:norms], refs[norms : norms + 2 * len(spans)]
     sent, held, norm, sems = refs[-4:]
     step = pl.program_id(0)
-
-    @pl.when(step == 0)
-    def _():
-        norm[...] = (norm_own[...] + norm_came[...]).astype(BF)
-
-    whole = held.shape[1] // 4
-    for rows, own, came in rows_of(refs[:-4]):
+    if norms:
+
+        @pl.when(step == 0)
+        def _():
+            norm[...] = (norm_parts[0][...] + norm_parts[1][...]).astype(BF)
+
+    for k, span in enumerate(spans):
+        own, came = parts[2 * k], parts[2 * k + 1]
         for second in range(2):
             for core in range(2):
-                row = (2 * second + core) * whole + rows.start
-                held[step, row : row + rows.stop - rows.start] = (
+                held[step, span.within(2 * second + core)] = (
                     own[0, second, 0, core] + came[0, second, 0, core]
                 )
-    send_block(step, held, sent, sems, (norm, sent.at[pl.ds(16 * whole, 16)]))
-
-
-def reduce_second_kernel(norm_own, norm_came, came_first, *refs):
-    sent, held, norm, sems = refs[-4:]
+    more = (norm, sent.at[pl.ds(16 * spans[0].of, 16)]) if norms else None
+    send_block(step, held, sent, sems, more)
+
+
+def reduce_second_kernel(spans, groups, norm_own, norm_came, *refs):
+    came_first, refs = refs[:groups], refs[groups:]
+    parts, refs = refs[: 2 * len(spans)], refs[2 * len(spans) :]
+    sent, held, (norm, *sems) = refs[:groups], refs[groups : 2 * groups], refs[2 * groups :]
     step = pl.program_id(0)
 
     @pl.when(step == 0)
     def _():
         norm[...] = (norm_own[...].astype(F32) + norm_came[...].astype(F32)).astype(BF)
 
-    whole = held.shape[1] // 2
-    for rows, own, came in rows_of(refs[:-4]):
+    for k, span in enumerate(spans):
+        own, came = parts[2 * k], parts[2 * k + 1]
         for core in range(2):
-            span = slice(core * whole + rows.start, core * whole + rows.stop)
-            held[step, span] = low_sum(own[0, 0, 0, core], came[0, 0, 0, core], came_first[span])
-    send_block(step, held, sent, sems, (norm, sent.at[pl.ds(8 * whole, 16)]))
-
-
-def reduce_third_kernel(norm_own, norm_came, place, came_first, came_second, *refs):
-    outs = refs[-4:]
+            rows = span.within(core)
+            held[span.group][step, rows] = low_sum(
+                own[0, 0, 0, core], came[0, 0, 0, core], came_first[span.group][rows]
+            )
+    for k in range(groups):
+        size = 4 * held[k].shape[1]
+        more = (norm, sent[k].at[pl.ds(size, 16)]) if k == groups - 1 else None
+        send_block(step, held[k], sent[k], sems[k], more)
+
+
+def reduce_third_kernel(spans, groups, norm_own, norm_came, place, *refs):
+    came_first, came_second, refs = refs[:groups], refs[groups : 2 * groups], refs[2 * groups :]
+    parts, outs = refs[:-4], refs[-4:]
     norm = (norm_own[...].astype(F32) + norm_came[...].astype(F32)).astype(BF)
-    whole = (outs[0].shape[0] - 16) // 2
+    rows = (outs[0].shape[0] - 16) // 2
     for d in range(4):
         z = (place[0] + d) & 3
-        outs[d][2 * whole :] = norm
-        for rows, own, came in rows_of(refs[:-4]):
+        outs[d][2 * rows :] = norm
+        for k, span in enumerate(spans):
+            own, came = parts[2 * k], parts[2 * k + 1]
             for core in range(2):
-                span = slice(core * whole + rows.start, core * whole + rows.stop)
-                size = rows.stop - rows.start
-                first = pl.multiple_of(z * 4 * whole + span.start, 16)
-                second = pl.multiple_of(z * 2 * whole + span.start, 16)
-                outs[d][span] = low_sum(
+                start = span.within(core).start
+                first = pl.multiple_of(z * 4 * span.of + start, 16)
+                second = pl.multiple_of(z * 2 * span.of + start, 16)
+                outs[d][span.overall(core, rows)] = low_sum(
                     own[0, 0, z, core],
                     came[0, 0, z, core],
-                    came_first[pl.ds(first, size)],
-                    came_second[pl.ds(second, size)],
+                    came_first[span.group][pl.ds(first, span.size)],
+                    came_second[span.group][pl.ds(second, span.size)],
                 )
 
 
@@ -1086,6 +1119,7 @@
 class Reduce:
     def __init__(self, order):
         self.order, self.own, self.came = order, [], []
+        self.spans, self.sent, self.first_came, self.rows = [], [], [], 0
 
     def add(self, own, other):
         self.own.append(own)
@@ -1098,8 +1132,8 @@
         self.norm = self.order.tie(norm)
         self.norm_came = to_core(self.norm)
 
-    def run(self, body, name, dims, operands, in_specs, part_spec, out_specs=None, scratch=(), grid=(4,)):
-        parts = [x for both in zip(self.own, self.came) for x in both]
+    def run(self, body, name, dims, operands, in_specs, part_spec, out_specs=None, scratch=(), grid=(4,), start=0):
+        parts = [x for both in zip(self.own[start:], self.came[start:]) for x in both]
         specs = [pl.BlockSpec(part_spec[0] + (part.shape[4], D), part_spec[1]) for part in parts]
         sent = small(
             self.order,
@@ -1114,45 +1148,62 @@
         )
         return [self.order.tie(x) for x in sent]
 
-    def first(self):
-        rows = self.rows = sum(own.shape[4] for own in self.own)
-        norm_spec = pl.BlockSpec((16, D), lambda i: (0, 0))
-        (self.first_sent,) = self.run(
-            reduce_first_kernel,
+    def held(self, dims):
+        return buffers([(dims, BF), ((16, D), BF)]) + [pltpu.SemaphoreType.DMA((5,))]
+
+    def first(self, norms=(), route=None):
+        start = len(self.spans)
+        sizes = [own.shape[4] for own in self.own[start:]]
+        rows, row, spans = sum(sizes), 0, []
+        for size in sizes:
+            spans.append(Span(len(self.sent), row, size, rows, self.rows + row))
+            row += size
+        self.spans += spans
+        self.rows += rows
+        (sent,) = self.run(
+            functools.partial(reduce_first_kernel, spans, len(norms)),
             "reduce_first",
-            [(16 * rows + 16, D)],
-            [self.norm, self.norm_came],
-            [norm_spec] * 2,
+            [(16 * rows + (16 if norms else 0), D)],
+            list(norms),
+            [pl.BlockSpec((16, D), lambda i: (0, 0))] * len(norms),
             ((1, 2, 1, 2), lambda i: (1, 0, i, 0, 0, 0)),
-            scratch=buffers([((4, 4 * rows, D), BF), ((16, D), BF)]) + [pltpu.SemaphoreType.DMA((5,))],
+            scratch=self.held((4, 4 * rows, D)),
+            start=start,
         )
-        self.first_came = to_yx(self.first_sent)
-
-    def second(self):
-        rows = self.rows
-        norm_spec = pl.BlockSpec((16, D), lambda i: (rows, 0))
-        (self.second_sent,) = self.run(
-            reduce_second_kernel,
+        self.sent.append(sent)
+        self.first_came.append((route or to_yx)(sent))
+
+    def last_rows(self, array):
+        block = array.shape[0] // 16 - 1
+        return pl.BlockSpec((16, D), lambda i: (block, 0))
+
+    def second(self, *routes):
+        groups = len(self.sent)
+        sizes = [self.spans[[span.group for span in self.spans].index(k)].of for k in range(groups)]
+        scratch = buffers([((4, 2 * size, D), BF) for size in sizes] + [((16, D), BF)])
+        self.second_sent = self.run(
+            functools.partial(reduce_second_kernel, self.spans, groups),
             "reduce_second",
-            [(8 * rows + 16, D)],
-            [self.first_sent, self.first_came, self.first_came],
-            [norm_spec] * 2 + [pl.BlockSpec((2 * rows, D), lambda i: (2 * i + 1, 0))],
+            [(8 * size + (16 if k == groups - 1 else 0), D) for k, size in enumerate(sizes)],
+            [self.sent[-1], self.first_came[-1]] + self.first_came,
+            [self.last_rows(self.sent[-1])] * 2
+            + [pl.BlockSpec((2 * size, D), lambda i: (2 * i + 1, 0)) for size in sizes],
             ((1, 1, 1, 2), lambda i: (0, 1, i, 0, 0, 0)),
-            scratch=buffers([((4, 2 * rows, D), BF), ((16, D), BF)]) + [pltpu.SemaphoreType.DMA((5,))],
+            scratch=scratch + [pltpu.SemaphoreType.DMA((5,))] * groups,
         )
-        self.second_came = to_xy(self.second_sent)
+        self.second_came = [route(sent) for route, sent in zip(routes, self.second_sent)]
 
     def third(self, place):
         rows = self.rows
-        norm_spec = pl.BlockSpec((16, D), lambda i: (rows // 2, 0))
+        came = self.first_came + self.second_came
         parts = self.run(
-            reduce_third_kernel,
+            functools.partial(reduce_third_kernel, self.spans, len(self.sent)),
             "reduce_third",
             [(2 * rows + 16, D)] * 4,
-            [self.second_sent, self.second_came, place, self.first_came, self.second_came],
-            [norm_spec] * 2
+            [self.second_sent[-1], self.second_came[-1], place] + came,
+            [self.last_rows(self.second_sent[-1])] * 2
             + [SM]
-            + [pl.BlockSpec(x.shape, lambda i: (0, 0)) for x in (self.first_came, self.second_came)],
+            + [pl.BlockSpec(x.shape, lambda i: (0, 0)) for x in came],
             ((1, 1, 4, 2), lambda i: (0, 0, 0, 0, 0, 0)),
             [pl.BlockSpec((2 * rows + 16, D), lambda i: (0, 0))] * 4,
             grid=(1,),
@@ -1360,7 +1411,7 @@
         one.done()
         gains = first_in
         w_self, w_enc = (Layout(0, 8), one.pieces), (Layout(32, 8), one.pieces)
-        w_enc_ffn = (Layout(0, 1), (whole,))
+        w_enc_ffn = (Layout(0, 1, 4), (whole,))
         w_cross = (Layout(256, 1, 1, 256, 384), (whole,))
     else:
         place = jnp.zeros((4,), jnp.int32)
@@ -1399,12 +1450,16 @@
     )
     if custom:
         red = Reduce(order)
-        red.add(*made_enc_ffn)
+        red.add(*made_enc_ffn[:2])
+        came = to_core(order.tie(made_enc_ffn[3]))
     grad_first, norm_self, *made_self = self_back(
         order, 4, place, gains, [first_in, second_in], grad_one, kept_self, w_self
     )
     if custom:
         red.arrive()
+        red.first((), to_dp)
+        red.own.append(made_enc_ffn[2])
+        red.came.append(order.tie(came))
         red.add(*made_self)
     grad_source, norm_total, *made_enc = self_back(
         order,
@@ -1418,11 +1473,12 @@
         (norm_enc_ffn, norm_self, norm_cross, norm_ffn),
     )
     if custom:
+        red.first_came[0] = order.tie(red.first_came[0])
         red.arrive()
         red.add(*made_enc)
         red.start_norm(norm_total)
-        red.first()
-        red.second()
+        red.first((red.norm, red.norm_came))
+        red.second(to_y, to_xy)
         red.third(place)
         scattered = order.tie(scattered)
         scattered_came = order.tie(to_dp(scattered))

time: 282 us -> 279 us (0.989)
  waiting for transfers between devices: 122 us -> 110 us
  starting transfers between devices: 37.7 us -> 42.1 us
  Pallas kernels: 105 us -> 109 us
    ppermute x1, waiting for transfers between devices: 36.7 us -> 20.1 us  [to_yx(): lax.ppermute(x, BOTH, route(lambda dp, z, y, core: (dp, z, y ^ 1, core) i...]
    ppermute x1, waiting for transfers between devices: 13.8 us -> 1.52 us  [to_xy(): lax.ppermute(x, BOTH, route(lambda dp, z, y, core: (dp ^ 1, z, y, core) i...]
    ppermute x2 -> x3, waiting for transfers between devices: 0.86 us -> 9.54 us  [to_y(): lax.ppermute(x, BOTH, route(lambda dp, z, y, core: (dp, z, 1 - y, core)))]
    ppermute x6 -> x7, waiting for transfers between devices: 20.6 us -> 25 us  [to_dp(): lax.ppermute(x, BOTH, route(lambda dp, z, y, core: (1 - dp, z, y, core)))]
    pallas_call x17 -> x18, Pallas kernels: 105 us -> 109 us  [call(): pl.pallas_call(ordered, name=name, out_shape=out_shape + [jax.ShapeDtypeS...]
    ppermute x9, waiting for transfers between devices: 40.9 us -> 44.9 us  [to_z(): lax.ppermute(x, BOTH, route(lambda dp, z, y, core: (dp, z + step, y, core)))]
    ppermute x6 -> x7, starting transfers between devices: 8.01 us -> 9.33 us  [to_dp(): lax.ppermute(x, BOTH, route(lambda dp, z, y, core: (1 - dp, z, y, core)))]
    ppermute x16 -> x17, waiting for transfers between devices: 8.3 us -> 8.31 us  [to_core(): lax.ppermute(x, BOTH, route(lambda dp, z, y, core: (dp, z, y, 1 - core)))]
  transfers between devices with their start and end apart: 37 -> 40, of which waited for: 19 -> 20; matrix products, arithmetic and copies ran while one was open for 0% -> 0% of each run, Pallas kernels for 27% -> 29%
where the time goes in v1:
time: 279 us; the launch traced here: 276 us
  waiting for transfers between devices  110 us (39%)
  Pallas kernels  109 us (39%)
  starting transfers between devices  42.1 us (15%)
  between operations  14.6 us (5%)
    pallas_call x18, Pallas kernels, call(): pl.pallas_call(ordered, name=name, out_shape=out_shape + [jax.ShapeDtypeS...  109 us
    ppermute x9, waiting for transfers between devices, to_z(): lax.ppermute(x, BOTH, route(lambda dp, z, y, core: (dp, z + step, y, core)))  44.9 us
    ppermute x7, waiting for transfers between devices, to_dp(): lax.ppermute(x, BOTH, route(lambda dp, z, y, core: (1 - dp, z, y, core)))  25 us
    ppermute x9, starting transfers between devices, to_z(): lax.ppermute(x, BOTH, route(lambda dp, z, y, core: (dp, z + step, y, core)))  21 us
    ppermute x1, waiting for transfers between devices, to_yx(): lax.ppermute(x, BOTH, route(lambda dp, z, y, core: (dp, z, y ^ 1, core) i...  20.1 us
    ppermute x3, waiting for transfers between devices, to_y(): lax.ppermute(x, BOTH, route(lambda dp, z, y, core: (dp, z, 1 - y, core)))  9.54 us
    ppermute x7, starting transfers between devices, to_dp(): lax.ppermute(x, BOTH, route(lambda dp, z, y, core: (1 - dp, z, y, core)))  9.33 us
    ppermute x17, waiting for transfers between devices, to_core(): lax.ppermute(x, BOTH, route(lambda dp, z, y, core: (dp, z, y, 1 - core)))  8.31 us
  transfers between devices with their start and end apart: 40, of which 20 were waited for; matrix products, arithmetic and copies ran while one was open for 0% of the time, Pallas kernels for 29%

profile of v1, /device:TPU:0, one launch (start us, length us, event | category | flops | bytes accessed | tf_op | source)
XLA Modules:
  0.0 275.9 jit_solution(12988215529229154454)
XLA Ops:
  7.2 2.2 pack.1
  9.4 0.5 collective-permute-start
  10.0 1.6 collective-permute-done.1.refs_4_
  11.7 1.9 pair_up.1
  13.5 4.8 %collective-permute-start.4 = (bf16[2,80,512]{2,1,0:T(8,128)(2,1)}, bf16[2,80,512]{2,1,0:T(8,128)(2,1)}, u32[]{:S(2)}, u32[]{:S(2)}) collective-permute-start(bf16[2,80,512]{2,1,0:T(8,128)(2,1)} %get-tuple-element.196.refs_1_), channel_id=1, source_target_pairs={{0,12},{1,13},{2,14},{3,15},{4,0},{5,1},{6,2},{7,3},{8,4},{9,5},{1... | collective-permute-start | bytes 491528 | tf_op jit(solution)/shard_map/ppermute | solution.py:804
  18.4 4.2 %collective-permute-done.4.refs_0_ = bf16[2,80,512]{2,1,0:T(8,128)(2,1)} collective-permute-done((bf16[2,80,512]{2,1,0:T(8,128)(2,1)}, bf16[2,80,512]{2,1,0:T(8,128)(2,1)}, u32[]{:S(2)}, u32[]{:S(2)}) %collective-permute-start.4) | collective-permute-done | bytes 163872 | tf_op jit(solution)/shard_map/ppermute | solution.py:804
  22.7 1.5 collective-permute-start.3
  24.2 3.4 %collective-permute-start.2 = (bf16[2,80,512]{2,1,0:T(8,128)(2,1)}, bf16[2,80,512]{2,1,0:T(8,128)(2,1)}, u32[]{:S(2)}, u32[]{:S(2)}) collective-permute-start(bf16[2,80,512]{2,1,0:T(8,128)(2,1)} %get-tuple-element.196.refs_1_), channel_id=1, source_target_pairs={{0,4},{1,5},{2,6},{3,7},{4,8},{5,9},{6,10},{7,11},{8,12},{9,13},{1... | collective-permute-start | bytes 491528 | tf_op jit(solution)/shard_map/ppermute | solution.py:804
  27.6 9.0 %collective-permute-done.3.refs_3_ = bf16[2,80,512]{2,1,0:T(8,128)(2,1)} collective-permute-done((bf16[2,80,512]{2,1,0:T(8,128)(2,1)}, bf16[2,80,512]{2,1,0:T(8,128)(2,1)}, u32[]{:S(2)}, u32[]{:S(2)}) %collective-permute-start.3) | collective-permute-done | bytes 163872 | tf_op jit(solution)/shard_map/ppermute | solution.py:804
  36.6 2.6 stack.2
  39.2 1.6 collective-permute-start.6
  40.8 1.5 collective-permute-start.5
  42.3 4.3 %collective-permute-start.8 = (bf16[2,64,512]{2,1,0:T(8,128)(2,1)}, bf16[2,64,512]{2,1,0:T(8,128)(2,1)}, u32[]{:S(2)}, u32[]{:S(2)}) collective-permute-start(bf16[2,64,512]{2,1,0:T(8,128)(2,1)} %get-tuple-element.207.refs_1_), channel_id=1, source_target_pairs={{0,8},{1,9},{2,10},{3,11},{4,12},{5,13},{6,14},{7,15},{8,0},{9,1},... | collective-permute-start | bytes 393224 | tf_op jit(solution)/shard_map/ppermute | solution.py:804
  46.6 2.0 collective-permute-start.7
  48.6 3.4 %collective-permute-done.9.refs_4_ = bf16[2,64,512]{2,1,0:T(8,128)(2,1)} collective-permute-done((bf16[2,64,512]{2,1,0:T(8,128)(2,1)}, bf16[2,64,512]{2,1,0:T(8,128)(2,1)}, u32[]{:S(2)}, u32[]{:S(2)}) %collective-permute-start.9) | collective-permute-done | bytes 131104 | tf_op jit(solution)/shard_map/ppermute | solution.py:804
  52.0 9.2 %collective-permute-done.8.refs_3_ = bf16[2,64,512]{2,1,0:T(8,128)(2,1)} collective-permute-done((bf16[2,64,512]{2,1,0:T(8,128)(2,1)}, bf16[2,64,512]{2,1,0:T(8,128)(2,1)}, u32[]{:S(2)}, u32[]{:S(2)}) %collective-permute-start.8) | collective-permute-done | bytes 131104 | tf_op jit(solution)/shard_map/ppermute | solution.py:804
  61.2 0.5 collective-permute-start.13
  61.7 1.4 collective-permute-start.10
  63.2 2.5 stack.3
  65.7 13.1 %collective-permute-done.10.refs_0_ = bf16[4,2,80,512]{3,2,1,0:T(8,128)(2,1)} collective-permute-done((bf16[4,2,80,512]{3,2,1,0:T(8,128)(2,1)}, bf16[4,2,80,512]{3,2,1,0:T(8,128)(2,1)}, u32[]{:S(2)}, u32[]{:S(2)}) %collective-permute-start.10) | collective-permute-done | bytes 655392 | tf_op jit(solution)/shard_map/ppermute | solution.py:816
  78.8 0.5 collective-permute-start.18
  79.3 1.3 collective-permute-start.16
  80.6 1.5 collective-permute-start.15
  82.0 10.5 %self_forward.1 = (f32[512,512]{1,0:T(8,128)}, bf16[512,512]{1,0:T(8,128)(2,1)}, bf16[512,1536]{1,0:T(8,128)(2,1)}, bf16[16,256,256]{2,1,0:T(8,128)(2,1)}, bf16[...) custom-call(s32[4]{0:T(128)} %get-tuple-element.190.refs_0_.refs_2_,, ...), custom_call_target="tpu_custom_call", output_to_operand_aliasing={{11}: (23, {})} | custom-call | flops 13210999808 | tf_op jit(solution)/shard_map/self_forward/pallas_call | solution.py:611
  92.5 0.9 collective-permute-done.16.refs_1_
  93.4 1.0 collective-permute-done.15.refs_0_
  94.4 1.5 collective-permute-start.17
  96.1 0.8 all-gather.2.cloned.1.call-done
  96.9 11.1 %second.1 = (bf16[256,512]{1,0:T(8,128)(2,1)}, bf16[256,2048]{1,0:T(8,128)(2,1)}, bf16[256,2048]{1,0:T(8,128)(2,1)}, bf16[256,512]{1,0:T(8,128)(2,1)}, bf16[512,...) custom-call(s32[4]{0:T(128)} %get-tuple-element.190.refs_0_.refs_2_,, ...), custom_call_target="tpu_custom_call", output_to_operand_aliasing={{10}: (8, {})} | custom-call | flops 14311000064 | tf_op jit(solution)/shard_map/second/pallas_call | solution.py:611
  108.1 1.0 collective-permute-done.17.refs_0_
  109.1 2.2 collective-permute-done.21.refs_0_
  111.3 21.4 %middle.1 = (f32[2,512]{1,0:T(2,128)}, f32[2,512]{1,0:T(2,128)}, bf16[256,512]{1,0:T(8,128)(2,1)}, bf16[256,512]{1,0:T(8,128)(2,1)}, f32[256,512]{1,0:T(8,128)},...) custom-call(s32[4]{0:T(128)} %get-tuple-element.190.refs_0_.refs_2_,, ...), custom_call_target="tpu_custom_call", output_to_operand_aliasing={{7}: (21, {})} | custom-call | flops 27510999040 | tf_op jit(solution)/shard_map/middle/pallas_call | solution.py:611
  132.8 10.2 %ffn_back.1 = (f32[256,512]{1,0:T(8,128)}, f32[2,512]{1,0:T(2,128)}, bf16[2,2,4,2,32,512]{5,4,3,2,1,0:T(8,128)(2,1)}, bf16[2,2,4,2,32,512]{5,4,3,2,1,0:T(8,128)(...) custom-call(s32[4]{0:T(128)} %get-tuple-element.190.refs_0_.refs_2_,, ...), custom_call_target="tpu_custom_call", output_to_operand_aliasing={{6}: (8, {})} | custom-call | flops 11230999552 | tf_op jit(solution)/shard_map/ffn_back/pallas_call | solution.py:611
  143.2 0.4 collective-permute-start.23
  143.6 13.3 %self_back.2 = (f32[256,512]{1,0:T(8,128)}, f32[2,512]{1,0:T(2,128)}, bf16[2,2,4,2,32,512]{5,4,3,2,1,0:T(8,128)(2,1)}, bf16[2,2,4,2,32,512]{5,4,3,2,1,0:T(8,128)(2,1)}, f32[8,128]{1,0:T(8,128)}) custom-call(s32[4]{0:T(128)} %get-tuple-element.190.refs_0_.refs_2_, f32[16,512]{1,0:T(8,128)} %get-tuple-element.225.refs_3_.refs_1_, ...), custom_call_target="tpu_custom_call", output_to_operand_aliasing={{4}: (17, {})} | custom-call | flops 13870999552 | tf_op jit(solution)/shard_map/self_back/pallas_call | solution.py:611
  156.9 2.9 %reduce_first.2 = (bf16[512,512]{1,0:T(8,128)(2,1)}, f32[8,128]{1,0:T(8,128)}) custom-call(bf16[2,2,4,2,32,512]{5,4,3,2,1,0:T(8,128)(2,1)} %get-tuple-element.277.refs_0_.refs_4_.refs_7_, bf16[2,2,4,2,32,512]{5,4,3,2,1,0:T(8,128)(2,1)} %get-tuple-element.280.refs_1_.refs_5_.refs_8_, f32[8,128]{1,0:T(8,128)} %get-tuple-element.281.refs_2_), custom_call_target="tpu_custom_call", output_to_operand_aliasing={{1}: (2, {})} | custom-call | flops 11000000 | tf_op jit(solution)/shard_map/reduce_first/pallas_call | solution.py:611
  160.1 1.4 collective-permute-start.25
  161.5 9.7 %self_back.3 = (f32[256,512]{1,0:T(8,128)}, f32[16,512]{1,0:T(8,128)}, bf16[2,2,4,2,32,512]{5,4,3,2,1,0:T(8,128)(2,1)}, bf16[2,2,4,2,32,512]{5,4,3,2,1,0:T(8,128)(2,1)}, f32[8,128]{1,0:T(8,128)}) custom-call(s32[4]{0:T(128)} %get-tuple-element.190.refs_0_.refs_2_, f32[16,512]{1,0:T(8,128)} %get-tuple-element.225.refs_3_.refs_1_, ...), custom_call_target="tpu_custom_call", output_to_operand_aliasing={{4}: (20, {})} | custom-call | flops 10131000320 | tf_op jit(solution)/shard_map/self_back/pallas_call | solution.py:611
  171.2 3.4 %collective-permute-done.25.refs_0_ = bf16[512,512]{1,0:T(8,128)(2,1)} collective-permute-done((bf16[512,512]{1,0:T(8,128)(2,1)}, bf16[512,512]{1,0:T(8,128)(2,1)}, u32[]{:S(2)}, u32[]{:S(2)}) %collective-permute-start.25) | collective-permute-done | bytes 524320 | tf_op jit(solution)/shard_map/ppermute | solution.py:816
  174.6 0.5 collective-permute-start.26
  175.1 2.5 collective-permute-done.26.refs_1_
  177.7 3.8 %reduce_first.3 = (bf16[1552,512]{1,0:T(8,128)(2,1)}, f32[8,128]{1,0:T(8,128)}) custom-call(f32[16,512]{1,0:T(8,128)} %get-tuple-element.297.refs_0_, f32[16,512]{1,0:T(8,128)} %collective-permute-done.26.refs_1_, bf16[2,2,4,2,32,512]{5,4,3,2,1,0:T(8,128)(2,1)} %get-tuple-element.298.refs_2_.refs_6_.refs_9_, ...), custom_call_target="tpu_custom_call", output_to_operand_aliasing={{1}: (8, {})} | custom-call | flops 11000000 | tf_op jit(solution)/shard_map/reduce_first/pallas_call | solution.py:611
  181.5 0.8 collective-permute-start.28
  182.4 20.1 %collective-permute-done.28.refs_1_.refs_3_.refs_4_ = bf16[1552,512]{1,0:T(8,128)(2,1)} collective-permute-done((bf16[1552,512]{1,0:T(8,128)(2,1)}, bf16[1552,512]{1,0:T(8,128)(2,1)}, u32[]{:S(2)}, u32[]{:S(2)}) %collective-permute-start.28) | collective-permute-done | bytes 1589280 | tf_op jit(solution)/shard_map/ppermute | solution.py:820
  202.5 4.3 %reduce_second.1 = (bf16[256,512]{1,0:T(8,128)(2,1)}, bf16[784,512]{1,0:T(8,128)(2,1)}, f32[8,128]{1,0:T(8,128)}) custom-call(bf16[1552,512]{1,0:T(8,128)(2,1)} %get-tuple-element.307.refs_0_, bf16[1552,512]{1,0:T(8,128)(2,1)} %collective-permute-done.28.refs_1_.refs_3_.refs_4_, ...), custom_call_target="tpu_custom_call", output_to_operand_aliasing={{2}: (12, {})} | custom-call | flops 11000000 | tf_op jit(solution)/shard_map/reduce_second/pallas_call | solution.py:611
  206.8 1.5 collective-permute-start.29
  208.3 0.9 collective-permute-start.30
  209.2 8.7 %collective-permute-done.30.refs_5_ = bf16[256,512]{1,0:T(8,128)(2,1)} collective-permute-done((bf16[256,512]{1,0:T(8,128)(2,1)}, bf16[256,512]{1,0:T(8,128)(2,1)}, u32[]{:S(2)}, u32[]{:S(2)}) %collective-permute-start.30) | collective-permute-done | bytes 262176 | tf_op jit(solution)/shard_map/ppermute | solution.py:812
  217.8 1.5 collective-permute-done.29.refs_1_.refs_6_
  219.3 3.9 %reduce_third.1 = (bf16[272,512]{1,0:T(8,128)(2,1)}, bf16[272,512]{1,0:T(8,128)(2,1)}, bf16[272,512]{1,0:T(8,128)(2,1)}, bf16[272,512]{1,0:T(8,128)(2,1)}, f32[8,128]{1,0:T(8,128)}) custom-call(bf16[784,512]{1,0:T(8,128)(2,1)} %get-tuple-element.314.refs_0_, ...), custom_call_target="tpu_custom_call", output_to_operand_aliasing={{4}: (15, {})} | custom-call | flops 11000000 | tf_op jit(solution)/shard_map/reduce_third/pallas_call | solution.py:611
  223.3 1.5 collective-permute-start.34
  224.7 2.3 collective-permute-start.33
  227.1 1.6 collective-permute-start.32
  228.6 1.0 collective-permute-start.31
  229.7 3.0 %collective-permute-done.34.refs_0_ = bf16[384,512]{1,0:T(8,128)(2,1)} collective-permute-done((bf16[384,512]{1,0:T(8,128)(2,1)}, bf16[384,512]{1,0:T(8,128)(2,1)}, u32[]{:S(2)}, u32[]{:S(2)}) %collective-permute-start.34) | collective-permute-done | bytes 393248 | tf_op jit(solution)/shard_map/ppermute | solution.py:816
  232.7 19.1 %collective-permute-done.32.refs_2_ = bf16[272,512]{1,0:T(8,128)(2,1)} collective-permute-done((bf16[272,512]{1,0:T(8,128)(2,1)}, bf16[272,512]{1,0:T(8,128)(2,1)}, u32[]{:S(2)}, u32[]{:S(2)}) %collective-permute-start.32) | collective-permute-done | bytes 278560 | tf_op jit(solution)/shard_map/ppermute | solution.py:804
  251.8 2.0 reduce_fourth.1
  253.8 2.4 collective-permute-start.36
  256.2 0.6 collective-permute-start.35
  256.8 2.0 spread.1
  258.8 2.5 norm_last.1
  261.3 3.5 %collective-permute-done.35.refs_0_ = bf16[2,128,512]{2,1,0:T(8,128)(2,1)} collective-permute-done((bf16[2,128,512]{2,1,0:T(8,128)(2,1)}, bf16[2,128,512]{2,1,0:T(8,128)(2,1)}, u32[]{:S(2)}, u32[]{:S(2)}) %collective-permute-start.35) | collective-permute-done | bytes 262176 | tf_op jit(solution)/shard_map/ppermute | solution.py:816
  264.8 1.9 collective-permute-done.37.refs_4_
  266.6 2.3 unpack.1
  (70 shorter events, 1.1 us)
Async XLA Ops:
  7.2 89.7 %all-gather.2.cloned.1.call-start = ((), (), s32[]{:S(2)}) async-start(), calls=%async_computation.1 | async-start | bytes 6684672 | tf_op jit(solution)/shard_map/all_gather | solution.py:1402
  9.4 2.2 collective-permute-start
  10.0 1.7 collective-permute-start.1
  13.5 9.0 %collective-permute-start.4 = (bf16[2,80,512]{2,1,0:T(8,128)(2,1)}, bf16[2,80,512]{2,1,0:T(8,128)(2,1)}, u32[]{:S(2)}, u32[]{:S(2)}) collective-permute-start(bf16[2,80,512]{2,1,0:T(8,128)(2,1)} %get-tuple-element.196.refs_1_), channel_id=1, source_target_pairs={{0,12},{1,13},{2,14},{3,15},{4,0},{5,1},{6,2},{7,3},{8,4},{9,5},{1... | collective-permute-start | bytes 491528 | tf_op jit(solution)/shard_map/ppermute | solution.py:804
  22.6 200.7 %reduce-scatter.2.cloned.1.call-start = ((), (), s32[]{:S(2)}) async-start(), calls=%async_computation.2 | async-start | bytes 6684672 | tf_op jit(solution)/shard_map/reduce_scatter | solution.py:1445
  22.7 14.0 %collective-permute-start.3 = (bf16[2,80,512]{2,1,0:T(8,128)(2,1)}, bf16[2,80,512]{2,1,0:T(8,128)(2,1)}, u32[]{:S(2)}, u32[]{:S(2)}) collective-permute-start(bf16[2,80,512]{2,1,0:T(8,128)(2,1)} %get-tuple-element.196.refs_1_), channel_id=1, source_target_pairs={{0,8},{1,9},{2,10},{3,11},{4,12},{5,13},{6,14},{7,15},{8,0},{9,1},... | collective-permute-start | bytes 491528 | tf_op jit(solution)/shard_map/ppermute | solution.py:804
  24.2 12.4 %collective-permute-start.2 = (bf16[2,80,512]{2,1,0:T(8,128)(2,1)}, bf16[2,80,512]{2,1,0:T(8,128)(2,1)}, u32[]{:S(2)}, u32[]{:S(2)}) collective-permute-start(bf16[2,80,512]{2,1,0:T(8,128)(2,1)} %get-tuple-element.196.refs_1_), channel_id=1, source_target_pairs={{0,4},{1,5},{2,6},{3,7},{4,8},{5,9},{6,10},{7,11},{8,12},{9,13},{1... | collective-permute-start | bytes 491528 | tf_op jit(solution)/shard_map/ppermute | solution.py:804
  39.2 22.0 %collective-permute-start.6 = (bf16[4,2,80,512]{3,2,1,0:T(8,128)(2,1)}, bf16[4,2,80,512]{3,2,1,0:T(8,128)(2,1)}, u32[]{:S(2)}, u32[]{:S(2)}) collective-permute-start(bf16[4,2,80,512]{3,2,1,0:T(8,128)(2,1)} %get-tuple-element.204.refs_7_.refs_15_.refs_9_.refs_12_), channel_id=1, source_target_pairs={{0,2},{1,3},{2,0},{3,1},{4,6},{5,7},{6,4},{7,5},{8,10},{9,11},{10,... | collective-permute-start | bytes 1966088 | tf_op jit(solution)/shard_map/ppermute | solution.py:812
  40.8 20.4 %collective-permute-start.5 = (bf16[4,2,80,512]{3,2,1,0:T(8,128)(2,1)}, bf16[4,2,80,512]{3,2,1,0:T(8,128)(2,1)}, u32[]{:S(2)}, u32[]{:S(2)}) collective-permute-start(bf16[4,2,80,512]{3,2,1,0:T(8,128)(2,1)} %get-tuple-element.204.refs_7_.refs_15_.refs_9_.refs_12_), channel_id=1, source_target_pairs={{0,16},{1,17},{2,18},{3,19},{4,20},{5,21},{6,22},{7,23},{8,24},{9,... | collective-permute-start | bytes 1966088 | tf_op jit(solution)/shard_map/ppermute | solution.py:816
  42.3 9.7 %collective-permute-start.9 = (bf16[2,64,512]{2,1,0:T(8,128)(2,1)}, bf16[2,64,512]{2,1,0:T(8,128)(2,1)}, u32[]{:S(2)}, u32[]{:S(2)}) collective-permute-start(bf16[2,64,512]{2,1,0:T(8,128)(2,1)} %get-tuple-element.207.refs_1_), channel_id=1, source_target_pairs={{0,12},{1,13},{2,14},{3,15},{4,0},{5,1},{6,2},{7,3},{8,4},{9,5},{1... | collective-permute-start | bytes 393224 | tf_op jit(solution)/shard_map/ppermute | solution.py:804
  42.3 18.9 %collective-permute-start.8 = (bf16[2,64,512]{2,1,0:T(8,128)(2,1)}, bf16[2,64,512]{2,1,0:T(8,128)(2,1)}, u32[]{:S(2)}, u32[]{:S(2)}) collective-permute-start(bf16[2,64,512]{2,1,0:T(8,128)(2,1)} %get-tuple-element.207.refs_1_), channel_id=1, source_target_pairs={{0,8},{1,9},{2,10},{3,11},{4,12},{5,13},{6,14},{7,15},{8,0},{9,1},... | collective-permute-start | bytes 393224 | tf_op jit(solution)/shard_map/ppermute | solution.py:804
  46.6 14.5 %collective-permute-start.7 = (bf16[2,64,512]{2,1,0:T(8,128)(2,1)}, bf16[2,64,512]{2,1,0:T(8,128)(2,1)}, u32[]{:S(2)}, u32[]{:S(2)}) collective-permute-start(bf16[2,64,512]{2,1,0:T(8,128)(2,1)} %get-tuple-element.207.refs_1_), channel_id=1, source_target_pairs={{0,4},{1,5},{2,6},{3,7},{4,8},{5,9},{6,10},{7,11},{8,12},{9,13},{1... | collective-permute-start | bytes 393224 | tf_op jit(solution)/shard_map/ppermute | solution.py:804
  52.0 13.7 %collective-permute-start.11 = (bf16[4,2,80,512]{3,2,1,0:T(8,128)(2,1)}, bf16[4,2,80,512]{3,2,1,0:T(8,128)(2,1)}, u32[]{:S(2)}, u32[]{:S(2)}) collective-permute-start(bf16[4,2,80,512]{3,2,1,0:T(8,128)(2,1)} %get-tuple-element.204.refs_7_.refs_15_.refs_9_.refs_12_), channel_id=1, source_target_pairs={{0,1},{1,0},{2,3},{3,2},{4,5},{5,4},{6,7},{7,6},{8,9},{9,8},{10,11... | collective-permute-start | bytes 1966088 | tf_op jit(solution)/shard_map/ppermute | solution.py:800
  61.2 4.5 %collective-permute-start.12 = (bf16[4,2,80,512]{3,2,1,0:T(8,128)(2,1)}, bf16[4,2,80,512]{3,2,1,0:T(8,128)(2,1)}, u32[]{:S(2)}, u32[]{:S(2)}) collective-permute-start(bf16[4,2,80,512]{3,2,1,0:T(8,128)(2,1)} %get-tuple-element.209.refs_8_.refs_16_.refs_10_.refs_13_), channel_id=1, source_target_pairs={{0,1},{1,0},{2,3},{3,2},{4,5},{5,4},{6,7},{7,6},{8,9},{9,8},{10,11... | collective-permute-start | bytes 1966088 | tf_op jit(solution)/shard_map/ppermute | solution.py:800
  61.2 4.5 %collective-permute-start.13 = (bf16[4,2,80,512]{3,2,1,0:T(8,128)(2,1)}, bf16[4,2,80,512]{3,2,1,0:T(8,128)(2,1)}, u32[]{:S(2)}, u32[]{:S(2)}) collective-permute-start(bf16[4,2,80,512]{3,2,1,0:T(8,128)(2,1)} %get-tuple-element.210.refs_9_.refs_17_.refs_11_.refs_14_), channel_id=1, source_target_pairs={{0,1},{1,0},{2,3},{3,2},{4,5},{5,4},{6,7},{7,6},{8,9},{9,8},{10,11... | collective-permute-start | bytes 1966088 | tf_op jit(solution)/shard_map/ppermute | solution.py:800
  61.7 17.0 %collective-permute-start.10 = (bf16[4,2,80,512]{3,2,1,0:T(8,128)(2,1)}, bf16[4,2,80,512]{3,2,1,0:T(8,128)(2,1)}, u32[]{:S(2)}, u32[]{:S(2)}) collective-permute-start(bf16[4,2,80,512]{3,2,1,0:T(8,128)(2,1)} %get-tuple-element.210.refs_9_.refs_17_.refs_11_.refs_14_), channel_id=1, source_target_pairs={{0,16},{1,17},{2,18},{3,19},{4,20},{5,21},{6,22},{7,23},{8,24},{9,... | collective-permute-start | bytes 1966088 | tf_op jit(solution)/shard_map/ppermute | solution.py:816
  78.8 3.3 %collective-permute-start.14 = (bf16[4,2,80,512]{3,2,1,0:T(8,128)(2,1)}, bf16[4,2,80,512]{3,2,1,0:T(8,128)(2,1)}, u32[]{:S(2)}, u32[]{:S(2)}) collective-permute-start(bf16[4,2,80,512]{3,2,1,0:T(8,128)(2,1)} %get-tuple-element.218.refs_10_.refs_18_.refs_12_.refs_15_), channel_id=1, source_target_pairs={{0,1},{1,0},{2,3},{3,2},{4,5},{5,4},{6,7},{7,6},{8,9},{9,8},{10,11... | collective-permute-start | bytes 1966088 | tf_op jit(solution)/shard_map/ppermute | solution.py:800
  78.8 29.3 %collective-permute-start.18 = (bf16[4,2,64,512]{3,2,1,0:T(8,128)(2,1)}, bf16[4,2,64,512]{3,2,1,0:T(8,128)(2,1)}, u32[]{:S(2)}, u32[]{:S(2)}) collective-permute-start(bf16[4,2,64,512]{3,2,1,0:T(8,128)(2,1)} %get-tuple-element.229.refs_13_), channel_id=1, source_target_pairs={{0,1},{1,0},{2,3},{3,2},{4,5},{5,4},{6,7},{7,6},{8,9},{9,8},{10,11... | collective-permute-start | bytes 1572872 | tf_op jit(solution)/shard_map/ppermute | solution.py:800
  79.3 14.1 %collective-permute-start.16 = (bf16[4,2,64,512]{3,2,1,0:T(8,128)(2,1)}, bf16[4,2,64,512]{3,2,1,0:T(8,128)(2,1)}, u32[]{:S(2)}, u32[]{:S(2)}) collective-permute-start(bf16[4,2,64,512]{3,2,1,0:T(8,128)(2,1)} %get-tuple-element.229.refs_13_), channel_id=1, source_target_pairs={{0,2},{1,3},{2,0},{3,1},{4,6},{5,7},{6,4},{7,5},{8,10},{9,11},{10,... | collective-permute-start | bytes 1572872 | tf_op jit(solution)/shard_map/ppermute | solution.py:812
  80.6 13.9 %collective-permute-start.15 = (bf16[4,2,64,512]{3,2,1,0:T(8,128)(2,1)}, bf16[4,2,64,512]{3,2,1,0:T(8,128)(2,1)}, u32[]{:S(2)}, u32[]{:S(2)}) collective-permute-start(bf16[4,2,64,512]{3,2,1,0:T(8,128)(2,1)} %get-tuple-element.229.refs_13_), channel_id=1, source_target_pairs={{0,16},{1,17},{2,18},{3,19},{4,20},{5,21},{6,22},{7,23},{8,24},{9,... | collective-permute-start | bytes 1572872 | tf_op jit(solution)/shard_map/ppermute | solution.py:816
  94.4 13.6 %collective-permute-start.20 = (bf16[4,2,64,512]{3,2,1,0:T(8,128)(2,1)}, bf16[4,2,64,512]{3,2,1,0:T(8,128)(2,1)}, u32[]{:S(2)}, u32[]{:S(2)}) collective-permute-start(bf16[4,2,64,512]{3,2,1,0:T(8,128)(2,1)} %get-tuple-element.240.refs_15_), channel_id=1, source_target_pairs={{0,1},{1,0},{2,3},{3,2},{4,5},{5,4},{6,7},{7,6},{8,9},{9,8},{10,11... | collective-permute-start | bytes 1572872 | tf_op jit(solution)/shard_map/ppermute | solution.py:800
  94.4 14.7 %collective-permute-start.17 = (bf16[4,2,64,512]{3,2,1,0:T(8,128)(2,1)}, bf16[4,2,64,512]{3,2,1,0:T(8,128)(2,1)}, u32[]{:S(2)}, u32[]{:S(2)}) collective-permute-start(bf16[4,2,64,512]{3,2,1,0:T(8,128)(2,1)} %get-tuple-element.240.refs_15_), channel_id=1, source_target_pairs={{0,16},{1,17},{2,18},{3,19},{4,20},{5,21},{6,22},{7,23},{8,24},{9,... | collective-permute-start | bytes 1572872 | tf_op jit(solution)/shard_map/ppermute | solution.py:816
  95.9 12.1 %collective-permute-start.19 = (bf16[4,2,64,512]{3,2,1,0:T(8,128)(2,1)}, bf16[4,2,64,512]{3,2,1,0:T(8,128)(2,1)}, u32[]{:S(2)}, u32[]{:S(2)}) collective-permute-start(bf16[4,2,64,512]{3,2,1,0:T(8,128)(2,1)} %get-tuple-element.239.refs_14_), channel_id=1, source_target_pairs={{0,1},{1,0},{2,3},{3,2},{4,5},{5,4},{6,7},{7,6},{8,9},{9,8},{10,11... | collective-permute-start | bytes 1572872 | tf_op jit(solution)/shard_map/ppermute | solution.py:800
  109.1 2.3 collective-permute-start.21
  143.0 16.8 %collective-permute-start.22 = (bf16[2,2,4,2,32,512]{5,4,3,2,1,0:T(8,128)(2,1)}, bf16[2,2,4,2,32,512]{5,4,3,2,1,0:T(8,128)(2,1)}, u32[]{:S(2)}, u32[]{:S(2)}) collective-permute-start(bf16[2,2,4,2,32,512]{5,4,3,2,1,0:T(8,128)(2,1)} %get-tuple-element.276), channel_id=1, source_target_pairs={{0,1},{1,0},{2,3},{3,2},{4,5},{5,4},{6,7},{7,6},{8,9},{9,8},{10,11... | collective-permute-start | bytes 3145736 | tf_op jit(solution)/shard_map/ppermute | solution.py:800
  143.2 13.6 %collective-permute-start.23 = (bf16[2,2,4,2,32,512]{5,4,3,2,1,0:T(8,128)(2,1)}, bf16[2,2,4,2,32,512]{5,4,3,2,1,0:T(8,128)(2,1)}, u32[]{:S(2)}, u32[]{:S(2)}) collective-permute-start(bf16[2,2,4,2,32,512]{5,4,3,2,1,0:T(8,128)(2,1)} %get-tuple-element.278), channel_id=1, source_target_pairs={{0,1},{1,0},{2,3},{3,2},{4,5},{5,4},{6,7},{7,6},{8,9},{9,8},{10,11... | collective-permute-start | bytes 3145736 | tf_op jit(solution)/shard_map/ppermute | solution.py:800
  159.9 14.7 %collective-permute-start.24 = (bf16[2,2,4,2,32,512]{5,4,3,2,1,0:T(8,128)(2,1)}, bf16[2,2,4,2,32,512]{5,4,3,2,1,0:T(8,128)(2,1)}, u32[]{:S(2)}, u32[]{:S(2)}) collective-permute-start(bf16[2,2,4,2,32,512]{5,4,3,2,1,0:T(8,128)(2,1)} %get-tuple-element.291), channel_id=1, source_target_pairs={{0,1},{1,0},{2,3},{3,2},{4,5},{5,4},{6,7},{7,6},{8,9},{9,8},{10,11... | collective-permute-start | bytes 3145736 | tf_op jit(solution)/shard_map/ppermute | solution.py:800
  160.1 14.5 %collective-permute-start.25 = (bf16[512,512]{1,0:T(8,128)(2,1)}, bf16[512,512]{1,0:T(8,128)(2,1)}, u32[]{:S(2)}, u32[]{:S(2)}) collective-permute-start(bf16[512,512]{1,0:T(8,128)(2,1)} %get-tuple-element.292), channel_id=1, source_target_pairs={{0,16},{1,17},{2,18},{3,19},{4,20},{5,21},{6,22},{7,23},{8,24},{9,... | collective-permute-start | bytes 1572872 | tf_op jit(solution)/shard_map/ppermute | solution.py:816
  174.6 3.1 %collective-permute-start.27 = (bf16[2,2,4,2,32,512]{5,4,3,2,1,0:T(8,128)(2,1)}, bf16[2,2,4,2,32,512]{5,4,3,2,1,0:T(8,128)(2,1)}, u32[]{:S(2)}, u32[]{:S(2)}) collective-permute-start(bf16[2,2,4,2,32,512]{5,4,3,2,1,0:T(8,128)(2,1)} %get-tuple-element.303), channel_id=1, source_target_pairs={{0,1},{1,0},{2,3},{3,2},{4,5},{5,4},{6,7},{7,6},{8,9},{9,8},{10,11... | collective-permute-start | bytes 3145736 | tf_op jit(solution)/shard_map/ppermute | solution.py:800
  174.6 3.0 %collective-permute-start.26 = (f32[16,512]{1,0:T(8,128)}, f32[16,512]{1,0:T(8,128)}, u32[]{:S(2)}, u32[]{:S(2)}) collective-permute-start(f32[16,512]{1,0:T(8,128)} %get-tuple-element.297.refs_0_), channel_id=1, source_target_pairs={{0,1},{1,0},{2,3},{3,2},{4,5},{5,4},{6,7},{7,6},{8,9},{9,8},{10,11... | collective-permute-start | bytes 98312 | tf_op jit(solution)/shard_map/ppermute | solution.py:800
  181.5 21.0 %collective-permute-start.28 = (bf16[1552,512]{1,0:T(8,128)(2,1)}, bf16[1552,512]{1,0:T(8,128)(2,1)}, u32[]{:S(2)}, u32[]{:S(2)}) collective-permute-start(bf16[1552,512]{1,0:T(8,128)(2,1)} %get-tuple-element.307.refs_0_), channel_id=1, source_target_pairs={{0,2},{1,17},{2,0},{3,19},{4,6},{5,21},{6,4},{7,23},{8,10},{9,25},... | collective-permute-start | bytes 4767752 | tf_op jit(solution)/shard_map/ppermute | solution.py:820
  206.8 12.5 %collective-permute-start.29 = (bf16[784,512]{1,0:T(8,128)(2,1)}, bf16[784,512]{1,0:T(8,128)(2,1)}, u32[]{:S(2)}, u32[]{:S(2)}) collective-permute-start(bf16[784,512]{1,0:T(8,128)(2,1)} %get-tuple-element.314.refs_0_), channel_id=1, source_target_pairs={{0,16},{1,3},{2,18},{3,1},{4,20},{5,7},{6,22},{7,5},{8,24},{9,11},... | collective-permute-start | bytes 2408456 | tf_op jit(solution)/shard_map/ppermute | solution.py:826
  208.3 9.6 %collective-permute-start.30 = (bf16[256,512]{1,0:T(8,128)(2,1)}, bf16[256,512]{1,0:T(8,128)(2,1)}, u32[]{:S(2)}, u32[]{:S(2)}) collective-permute-start(bf16[256,512]{1,0:T(8,128)(2,1)} %get-tuple-element.315), channel_id=1, source_target_pairs={{0,2},{1,3},{2,0},{3,1},{4,6},{5,7},{6,4},{7,5},{8,10},{9,11},{10,... | collective-permute-start | bytes 786440 | tf_op jit(solution)/shard_map/ppermute | solution.py:812
  223.3 9.4 %collective-permute-start.34 = (bf16[384,512]{1,0:T(8,128)(2,1)}, bf16[384,512]{1,0:T(8,128)(2,1)}, u32[]{:S(2)}, u32[]{:S(2)}) collective-permute-start(bf16[384,512]{1,0:T(8,128)(2,1)} %get-tuple-element.331.refs_0_), channel_id=1, source_target_pairs={{0,16},{1,17},{2,18},{3,19},{4,20},{5,21},{6,22},{7,23},{8,24},{9,... | collective-permute-start | bytes 1179656 | tf_op jit(solution)/shard_map/ppermute | solution.py:816
  224.7 8.0 %collective-permute-start.33 = (bf16[272,512]{1,0:T(8,128)(2,1)}, bf16[272,512]{1,0:T(8,128)(2,1)}, u32[]{:S(2)}, u32[]{:S(2)}) collective-permute-start(bf16[272,512]{1,0:T(8,128)(2,1)} %get-tuple-element.328), channel_id=1, source_target_pairs={{0,12},{1,13},{2,14},{3,15},{4,0},{5,1},{6,2},{7,3},{8,4},{9,5},{1... | collective-permute-start | bytes 835592 | tf_op jit(solution)/shard_map/ppermute | solution.py:804
  227.1 24.7 %collective-permute-start.32 = (bf16[272,512]{1,0:T(8,128)(2,1)}, bf16[272,512]{1,0:T(8,128)(2,1)}, u32[]{:S(2)}, u32[]{:S(2)}) collective-permute-start(bf16[272,512]{1,0:T(8,128)(2,1)} %get-tuple-element.325), channel_id=1, source_target_pairs={{0,8},{1,9},{2,10},{3,11},{4,12},{5,13},{6,14},{7,15},{8,0},{9,1},... | collective-permute-start | bytes 835592 | tf_op jit(solution)/shard_map/ppermute | solution.py:804
  228.6 23.2 %collective-permute-start.31 = (bf16[272,512]{1,0:T(8,128)(2,1)}, bf16[272,512]{1,0:T(8,128)(2,1)}, u32[]{:S(2)}, u32[]{:S(2)}) collective-permute-start(bf16[272,512]{1,0:T(8,128)(2,1)} %get-tuple-element.322), channel_id=1, source_target_pairs={{0,4},{1,5},{2,6},{3,7},{4,8},{5,9},{6,10},{7,11},{8,12},{9,13},{1... | collective-permute-start | bytes 835592 | tf_op jit(solution)/shard_map/ppermute | solution.py:804
  253.8 7.4 %collective-permute-start.36 = (bf16[2,128,512]{2,1,0:T(8,128)(2,1)}, bf16[2,128,512]{2,1,0:T(8,128)(2,1)}, u32[]{:S(2)}, u32[]{:S(2)}) collective-permute-start(bf16[2,128,512]{2,1,0:T(8,128)(2,1)} %get-tuple-element.336.refs_1_), channel_id=1, source_target_pairs={{0,1},{1,0},{2,3},{3,2},{4,5},{5,4},{6,7},{7,6},{8,9},{9,8},{10,11... | collective-permute-start | bytes 786440 | tf_op jit(solution)/shard_map/ppermute | solution.py:800
  256.2 8.5 %collective-permute-start.35 = (bf16[2,128,512]{2,1,0:T(8,128)(2,1)}, bf16[2,128,512]{2,1,0:T(8,128)(2,1)}, u32[]{:S(2)}, u32[]{:S(2)}) collective-permute-start(bf16[2,128,512]{2,1,0:T(8,128)(2,1)} %get-tuple-element.336.refs_1_), channel_id=1, source_target_pairs={{0,16},{1,17},{2,18},{3,19},{4,20},{5,21},{6,22},{7,23},{8,24},{9,... | collective-permute-start | bytes 786440 | tf_op jit(solution)/shard_map/ppermute | solution.py:816
  264.8 1.9 collective-permute-start.37
Sparse Core Ops, SparseCore 0:
  22.7 74.1 all-gather.1
  132.9 85.8 reduce-scatter.1
